TPU v7x, 32 devices: a whole 2x2x4 slice. The times are simulated.
32 devices in a mesh: groups: 2 (over y), blk: 8 (over z, x), shard: 2 (over core).
Axes of the slice: x: 2, y: 2, z: 4, core: 2. Of those that a mesh axis runs over, the one named last changes fastest.
Arguments:
- queries: bfloat16 [8192, 768], P(('groups', 'blk')), parts along dimension 0, may hold values from -8 to 8
- passages: bfloat16 [512, 768], P(('groups', 'blk', 'shard')), parts along dimension 0, may hold values from -8 to 8
- cand_ids: int32 [8192, 32], P(('groups', 'blk')), parts along dimension 0, may hold values from 0 to 255
Outputs:
- soft_labels: float32 [8192, 32], P(('groups', 'blk')), parts along dimension 0
There are 2 independent parts, one for each index of `groups`. A program takes and returns all parts, laid end to end along the dimension named above; each array names one. Nothing has to cross between parts.
All inputs are finite; a program needn't handle non-finite values.
Results may differ from a plain program's by a relative error of at most 0.0003.
Values may be sent and summed in bfloat16 or wider, within the bound.
No kernel may reach another device: no remote copies, remote signals or barrier semaphores. Data moves between devices by JAX's collectives and lax.ppermute only.
A program may use at most 64 MiB of HBM per device.

v0:
```python
import math

import jax
import jax.numpy as jnp
from jax import lax
from jax.sharding import PartitionSpec as P

SCALE = 0.2


def merged(part, axis, combine):
    gathered = jax.tree.map(lambda a: lax.all_gather(a, axis), part)

    def take(source):
        return jax.tree.map(lambda a: lax.dynamic_index_in_dim(a, source, 0, False), gathered)

    return lax.fori_loop(
        1, lax.axis_size(axis), lambda source, state: combine(state, take(source)), take(0)
    )


def combine(first, second):
    top = jnp.maximum(first[0], second[0])
    total = first[1] * jnp.exp(first[0] - top) + second[1] * jnp.exp(second[0] - top)
    return (top, total, first[2] + second[2])


def block_stats(block, piece):
    logits = SCALE * lax.dot_general(
        block, piece, (((1,), (1,)), ((), ())), preferred_element_type=jnp.float32
    )
    piece_top = jnp.max(logits, axis=1)
    piece_sum = jnp.sum(jnp.exp(logits - piece_top[:, None]), axis=1)
    return (logits, piece_top, piece_sum)


def pick_rows(queries, corpus_rows, where_ids):
    height = corpus_rows.shape[0]
    total = queries.shape[0]
    group = math.gcd(total, 32)
    qgroups = queries.reshape(total // group, group, queries.shape[1])
    igroups = where_ids.reshape(total // group, group, where_ids.shape[1])

    def one_group(pair):
        block, ids = pair
        chosen = jnp.take(corpus_rows, jnp.clip(ids, 0, height - 1), axis=0)
        values = SCALE * jnp.einsum("qd,qkd->qk", block, chosen, preferred_element_type=jnp.float32)
        return jnp.where(ids >= 0, values, 0.0)

    return lax.map(one_group, (qgroups, igroups)).reshape(total, where_ids.shape[1])


def body(queries, passages, cand_ids):
    rows = passages.shape[0]
    n_shard = lax.axis_size("shard")
    own = lax.axis_index("shard")
    owner = cand_ids // rows % n_shard
    gathered_index = cand_ids // (rows * n_shard) * rows + cand_ids % rows
    where_ids = jnp.where(owner == own, gathered_index, -1)
    count_q = queries.shape[0]
    corpus_rows = lax.all_gather(passages, "blk", axis=0, tiled=True)
    height = corpus_rows.shape[0]
    width = math.gcd(height, 1024)
    start_pair = (jnp.full((count_q,), -1e30, jnp.float32), jnp.zeros((count_q,), jnp.float32))

    def step_block(index, carry):
        piece = lax.dynamic_slice_in_dim(corpus_rows, index * width, width, 0)
        logits, piece_top, piece_sum = block_stats(queries, piece)
        top = jnp.maximum(carry[0], piece_top)
        total = carry[1] * jnp.exp(carry[0] - top) + piece_sum * jnp.exp(piece_top - top)
        return (top, total)

    top_now, sum_now = lax.fori_loop(0, height // width, step_block, start_pair)
    picked_now = pick_rows(queries, corpus_rows, where_ids)
    partial_state = (top_now, sum_now, picked_now)
    top, total, picked = merged(partial_state, "shard", combine)
    return picked - (top + jnp.log(total))[:, None]


def solution(mesh):
    return jax.shard_map(
        body,
        mesh=mesh,
        in_specs=(
            P(("groups", "blk"), None),
            P(("groups", "blk", "shard"), None),
            P(("groups", "blk"), None),
        ),
        out_specs=P(("groups", "blk"), None),
        check_vma=False,
    )
```

profile of v0, /device:TPU:0, one launch (start us, length us, event | category | flops | bytes accessed | tf_op | source)
XLA Modules:
  0.0 130.1 jit_solution(3999854779597158002)
XLA Ops:
  0.0 1.0 fusion.11
  1.0 32.6 %all_gather.14 = bf16[128,768]{1,0:T(8,128)(2,1)S(1)} all-gather(bf16[16,768]{1,0:T(8,128)(2,1)} %param.6), channel_id=1, replica_groups=mesh['groups'=2,'blk'=8,'shard'=2] {'blk'}, dimensions={0}, use_global_device_ids=true | all-gather | bytes 221184 | tf_op jit(solution)/shard_map/all_gather | solution.py:61
  33.7 88.5 %while.2 = (s32[]{:T(128)}, f32[16,32,32]{2,1,0:T(8,128)S(1)}, s32[16,32,32]{2,1,0:T(8,128)S(1)}, bf16[16,32,768]{2,1,0:T(8,128)(2,1)}, bf16[128,768]{1,0:T(8,128)(2,1)S(1)}, /*index=5*/s32[]{:T(128)}) while((s32[]{:T(128)}, f32[16,32,32]{2,1,0:T(8,128)S(1)}, s32[16,32,32]{2,1,0:T(8,128)S(1)}, bf16[16,32,768]{2,1,0:T(8,128)(2,1)}, ...), condition=%wide.region_1.2_spmd, body=%wide.region_0.1_spmd.sunk | while | flops 2374658 | bytes 4954205 | solution.py:50
  33.9 0.8 dynamic-slice_bitcast_fusion.2
  34.7 4.0 %gather_fusion = bf16[1024,768]{1,0:T(8,128)(2,1)S(1)} fusion(bf16[128,768]{1,0:T(8,128)(2,1)S(1)} %get-tuple-element.140, s32[1024]{0:T(1024)S(1)} %broadcast_clamp_fusion.2), kind=kCustom, calls=%fused_computation.clone.1 | custom fusion | bytes 3149824 | tf_op jit(solution)/shard_map/while/body/eval_jaxpr/jit(_take)/gather | solution.py:46
  40.2 4.0 %gather_fusion = bf16[1024,768]{1,0:T(8,128)(2,1)S(1)} fusion(bf16[128,768]{1,0:T(8,128)(2,1)S(1)} %get-tuple-element.140, s32[1024]{0:T(1024)S(1)} %broadcast_clamp_fusion.2), kind=kCustom, calls=%fused_computation.clone.1 | custom fusion | bytes 3149824 | tf_op jit(solution)/shard_map/while/body/eval_jaxpr/jit(_take)/gather | solution.py:46
  45.7 4.0 %gather_fusion = bf16[1024,768]{1,0:T(8,128)(2,1)S(1)} fusion(bf16[128,768]{1,0:T(8,128)(2,1)S(1)} %get-tuple-element.140, s32[1024]{0:T(1024)S(1)} %broadcast_clamp_fusion.2), kind=kCustom, calls=%fused_computation.clone.1 | custom fusion | bytes 3149824 | tf_op jit(solution)/shard_map/while/body/eval_jaxpr/jit(_take)/gather | solution.py:46
  51.3 4.0 %gather_fusion = bf16[1024,768]{1,0:T(8,128)(2,1)S(1)} fusion(bf16[128,768]{1,0:T(8,128)(2,1)S(1)} %get-tuple-element.140, s32[1024]{0:T(1024)S(1)} %broadcast_clamp_fusion.2), kind=kCustom, calls=%fused_computation.clone.1 | custom fusion | bytes 3149824 | tf_op jit(solution)/shard_map/while/body/eval_jaxpr/jit(_take)/gather | solution.py:46
  56.8 4.0 %gather_fusion = bf16[1024,768]{1,0:T(8,128)(2,1)S(1)} fusion(bf16[128,768]{1,0:T(8,128)(2,1)S(1)} %get-tuple-element.140, s32[1024]{0:T(1024)S(1)} %broadcast_clamp_fusion.2), kind=kCustom, calls=%fused_computation.clone.1 | custom fusion | bytes 3149824 | tf_op jit(solution)/shard_map/while/body/eval_jaxpr/jit(_take)/gather | solution.py:46
  62.3 4.0 %gather_fusion = bf16[1024,768]{1,0:T(8,128)(2,1)S(1)} fusion(bf16[128,768]{1,0:T(8,128)(2,1)S(1)} %get-tuple-element.140, s32[1024]{0:T(1024)S(1)} %broadcast_clamp_fusion.2), kind=kCustom, calls=%fused_computation.clone.1 | custom fusion | bytes 3149824 | tf_op jit(solution)/shard_map/while/body/eval_jaxpr/jit(_take)/gather | solution.py:46
  67.9 4.0 %gather_fusion = bf16[1024,768]{1,0:T(8,128)(2,1)S(1)} fusion(bf16[128,768]{1,0:T(8,128)(2,1)S(1)} %get-tuple-element.140, s32[1024]{0:T(1024)S(1)} %broadcast_clamp_fusion.2), kind=kCustom, calls=%fused_computation.clone.1 | custom fusion | bytes 3149824 | tf_op jit(solution)/shard_map/while/body/eval_jaxpr/jit(_take)/gather | solution.py:46
  73.4 4.0 %gather_fusion = bf16[1024,768]{1,0:T(8,128)(2,1)S(1)} fusion(bf16[128,768]{1,0:T(8,128)(2,1)S(1)} %get-tuple-element.140, s32[1024]{0:T(1024)S(1)} %broadcast_clamp_fusion.2), kind=kCustom, calls=%fused_computation.clone.1 | custom fusion | bytes 3149824 | tf_op jit(solution)/shard_map/while/body/eval_jaxpr/jit(_take)/gather | solution.py:46
  78.9 4.0 %gather_fusion = bf16[1024,768]{1,0:T(8,128)(2,1)S(1)} fusion(bf16[128,768]{1,0:T(8,128)(2,1)S(1)} %get-tuple-element.140, s32[1024]{0:T(1024)S(1)} %broadcast_clamp_fusion.2), kind=kCustom, calls=%fused_computation.clone.1 | custom fusion | bytes 3149824 | tf_op jit(solution)/shard_map/while/body/eval_jaxpr/jit(_take)/gather | solution.py:46
  84.5 4.0 %gather_fusion = bf16[1024,768]{1,0:T(8,128)(2,1)S(1)} fusion(bf16[128,768]{1,0:T(8,128)(2,1)S(1)} %get-tuple-element.140, s32[1024]{0:T(1024)S(1)} %broadcast_clamp_fusion.2), kind=kCustom, calls=%fused_computation.clone.1 | custom fusion | bytes 3149824 | tf_op jit(solution)/shard_map/while/body/eval_jaxpr/jit(_take)/gather | solution.py:46
  90.0 4.0 %gather_fusion = bf16[1024,768]{1,0:T(8,128)(2,1)S(1)} fusion(bf16[128,768]{1,0:T(8,128)(2,1)S(1)} %get-tuple-element.140, s32[1024]{0:T(1024)S(1)} %broadcast_clamp_fusion.2), kind=kCustom, calls=%fused_computation.clone.1 | custom fusion | bytes 3149824 | tf_op jit(solution)/shard_map/while/body/eval_jaxpr/jit(_take)/gather | solution.py:46
  95.5 4.0 %gather_fusion = bf16[1024,768]{1,0:T(8,128)(2,1)S(1)} fusion(bf16[128,768]{1,0:T(8,128)(2,1)S(1)} %get-tuple-element.140, s32[1024]{0:T(1024)S(1)} %broadcast_clamp_fusion.2), kind=kCustom, calls=%fused_computation.clone.1 | custom fusion | bytes 3149824 | tf_op jit(solution)/shard_map/while/body/eval_jaxpr/jit(_take)/gather | solution.py:46
  101.1 4.0 %gather_fusion = bf16[1024,768]{1,0:T(8,128)(2,1)S(1)} fusion(bf16[128,768]{1,0:T(8,128)(2,1)S(1)} %get-tuple-element.140, s32[1024]{0:T(1024)S(1)} %broadcast_clamp_fusion.2), kind=kCustom, calls=%fused_computation.clone.1 | custom fusion | bytes 3149824 | tf_op jit(solution)/shard_map/while/body/eval_jaxpr/jit(_take)/gather | solution.py:46
  106.6 4.0 %gather_fusion = bf16[1024,768]{1,0:T(8,128)(2,1)S(1)} fusion(bf16[128,768]{1,0:T(8,128)(2,1)S(1)} %get-tuple-element.140, s32[1024]{0:T(1024)S(1)} %broadcast_clamp_fusion.2), kind=kCustom, calls=%fused_computation.clone.1 | custom fusion | bytes 3149824 | tf_op jit(solution)/shard_map/while/body/eval_jaxpr/jit(_take)/gather | solution.py:46
  112.1 4.0 %gather_fusion = bf16[1024,768]{1,0:T(8,128)(2,1)S(1)} fusion(bf16[128,768]{1,0:T(8,128)(2,1)S(1)} %get-tuple-element.140, s32[1024]{0:T(1024)S(1)} %broadcast_clamp_fusion.2), kind=kCustom, calls=%fused_computation.clone.1 | custom fusion | bytes 3149824 | tf_op jit(solution)/shard_map/while/body/eval_jaxpr/jit(_take)/gather | solution.py:46
  117.7 4.0 %gather_fusion = bf16[1024,768]{1,0:T(8,128)(2,1)S(1)} fusion(bf16[128,768]{1,0:T(8,128)(2,1)S(1)} %get-tuple-element.140, s32[1024]{0:T(1024)S(1)} %broadcast_clamp_fusion.2), kind=kCustom, calls=%fused_computation.clone.1 | custom fusion | bytes 3149824 | tf_op jit(solution)/shard_map/while/body/eval_jaxpr/jit(_take)/gather | solution.py:46
  122.4 1.9 %all_gather.15 = f32[2,512,32]{1,2,0:T(8,128)S(1)} all-gather(f32[1,512,32]{1,2,0:T(8,128)S(1)} %copy.10), channel_id=1, replica_groups=mesh['groups'=2,'blk'=8,'shard'=2] {'shard'}, dimensions={0}, use_global_device_ids=true | all-gather | bytes 196608 | tf_op jit(solution)/shard_map/all_gather | solution.py:12
  124.3 1.5 %fusion.22 = (f32[512]{0:T(512)S(1)}, f32[512,128]{0,1:T(8,128)S(1)}) fusion(bf16[512,768]{1,0:T(8,128)(2,1)} %bitcast.53, bf16[128,768]{1,0:T(8,128)(2,1)S(1)} %get-tuple-element.142), kind=kOutput, calls=%fused_computation.48 | convolution fusion | flops 100793856 | bytes 1247232 | tf_op jit(solution)/shard_map/while/body/eval_jaxpr/dot_general | solution.py:29
  125.9 1.8 %all-gather = f32[2,1,512]{2,1,0:T(1,128)S(1)} all-gather(f32[1,1,512]{2,1,0:T(1,128)S(1)} %get-tuple-element.89), channel_id=1, replica_groups=mesh['groups'=2,'blk'=8,'shard'=2] {'shard'}, dimensions={0}, use_global_device_ids=true | all-gather | bytes 6144 | tf_op jit(solution)/shard_map/all_gather | solution.py:12
  127.7 1.8 %all-gather.1 = f32[2,1,512]{2,1,0:T(1,128)S(1)} all-gather(f32[1,1,512]{2,1,0:T(1,128)S(1)} %get-tuple-element.90), channel_id=1, replica_groups=mesh['groups'=2,'blk'=8,'shard'=2] {'shard'}, dimensions={0}, use_global_device_ids=true | all-gather | bytes 6144 | tf_op jit(solution)/shard_map/all_gather | solution.py:12
  (120 shorter events, 24.3 us)
where the time goes:
time: 131 us; the launch traced here: 130 us
  local copies, waits for them, and re-layouts  78.2 us (60%)
  blocking collectives  38.1 us (29%)
  matrix products  10.9 us (8%)
  other arithmetic  2.53 us (2%)
    gather x16, local copies, waits for them, and re-layouts, one_group(): chosen = jnp.take(corpus_rows, jnp.clip(ids, 0, height - 1), axis=0)  63.9 us
    all_gather x1, blocking collectives, body(): corpus_rows = lax.all_gather(passages, 'blk', axis=0, tiled=True)  32.6 us
    squeeze x16, local copies, waits for them, and re-layouts, pick_rows(): lax.map(one_group, (qgroups, igroups)).reshape(total, where_ids.shape[1])  12.9 us
    dot_general x16, matrix products, one_group(): jnp.einsum('qd,qkd->qk', block, chosen, preferred_element_type=jnp.float32)  9.34 us
    all_gather x3, blocking collectives, merged(): gathered = jax.tree.map(lambda a: lax.all_gather(a, axis), part)  5.46 us

commit v1 on v0

v1 whole, which is shorter than its diff:
```python
import functools

import jax
import jax.numpy as jnp
from jax import lax
from jax.experimental import pallas as pl
from jax.experimental.pallas import tpu as pltpu
from jax.sharding import PartitionSpec as P

SCALE = 0.2
AXES = ("blk", "shard")
BLOCK = 256


def parity(value):
    return value.bit_count() & 1


def step_masks(n_blk, kind):
    bits = n_blk.bit_length() - 1
    masks = [(2 << bit) | 1 for bit in range(bits - 1, -1, -1)]
    if bits >= 2 and kind:
        masks[-1], masks[-2] = masks[-2], masks[-1]
    return masks + [1]


def kind_mask(n_blk):
    return 0b111 if n_blk >= 4 else 0


def places(masks):
    reach = {0: 0}
    for step, mask in enumerate(masks):
        reach |= {source ^ mask: place | (1 << step) for source, place in reach.items()}
    return [reach[1 << bit] for bit in range(len(masks))]


def logits_of(rows, queries):
    return SCALE * lax.dot_general(
        rows, queries, (((1,), (1,)), ((), ())), preferred_element_type=jnp.float32
    )


def picked_in(logits, ids, start, before):
    chosen = []
    for top in range(0, ids.shape[0], 8):
        local = ids[top : top + 8] - start
        chunk, row = local >> 3, local & 7
        value = before[top : top + 8]
        for c in range(logits.shape[0] // 8):
            found = jnp.take_along_axis(
                logits[c * 8 : c * 8 + 8], row, axis=0, mode="promise_in_bounds"
            )
            value = jnp.where(chunk == c, found, value)
        chosen.append(value)
    return jnp.concatenate(chosen, axis=0)


def label_kernel(rows, n_blk, q_ref, own_ref, other_ref, ids_ref, out_ref, logits_ref):
    me = lax.axis_index("blk") * 2 + lax.axis_index("shard")
    kind = jnp.int32(0)
    for bit in range(kind_mask(n_blk).bit_length()):
        kind = kind ^ ((me >> bit) & 1)
    ids = ids_ref[...]
    shift = rows.bit_length() - 1
    source = (ids >> shift) ^ me
    tables = [places(step_masks(n_blk, other)) for other in (0, 1)]
    found = []
    for table in tables:
        place = jnp.zeros_like(ids)
        for bit, added in enumerate(table):
            place = place ^ (((source >> bit) & 1) * added)
        found.append(place)
    theirs = found[0] >> (len(tables[0]) - 1)
    flips = parity(kind_mask(n_blk) & 1)
    place = jnp.where((kind ^ (theirs * flips)) == 0, found[0], found[1])
    local = (place << shift) | (ids & (rows - 1))

    half = own_ref.shape[0]
    zero = jnp.zeros(ids.shape, jnp.float32)
    if half * 2 <= BLOCK:
        first = logits_of(own_ref[...], q_ref[...])
        second = logits_of(other_ref[...], q_ref[...])
        top = jnp.maximum(
            jnp.max(first, axis=0, keepdims=True), jnp.max(second, axis=0, keepdims=True)
        )
        total = jnp.sum(jnp.exp(first - top), axis=0, keepdims=True) + jnp.sum(
            jnp.exp(second - top), axis=0, keepdims=True
        )
        picked = picked_in(second, local, half, picked_in(first, local, 0, zero))
        out_ref[...] = picked - (top + jnp.log(total))
        return

    steps = half // BLOCK

    def fill(index, top):
        at = pl.multiple_of(index * BLOCK, BLOCK)
        first = logits_of(own_ref[pl.ds(at, BLOCK)], q_ref[...])
        second = logits_of(other_ref[pl.ds(at, BLOCK)], q_ref[...])
        logits_ref[pl.ds(at, BLOCK)] = first
        logits_ref[pl.ds(pl.multiple_of(half + at, BLOCK), BLOCK)] = second
        return jnp.maximum(
            top,
            jnp.maximum(
                jnp.max(first, axis=0, keepdims=True), jnp.max(second, axis=0, keepdims=True)
            ),
        )

    top = lax.fori_loop(0, steps, fill, jnp.full((1, ids.shape[1]), -jnp.inf, jnp.float32))

    def read(index, carry):
        total, picked = carry
        at = pl.multiple_of(index * BLOCK, BLOCK)
        block = logits_ref[pl.ds(at, BLOCK)]
        total = total + jnp.sum(jnp.exp(block - top), axis=0, keepdims=True)
        return (total, picked_in(block, local, at, picked))

    total, picked = lax.fori_loop(0, 2 * steps, read, (jnp.zeros_like(top), zero))
    out_ref[...] = picked - (top + jnp.log(total))


def body(queries, passages, cand_ids):
    rows = passages.shape[0]
    n_blk = lax.axis_size("blk")
    n_all = 2 * n_blk
    mix = kind_mask(n_blk)
    tables = [step_masks(n_blk, kind) for kind in (0, 1)]
    held = passages
    for step in range(len(tables[0]) - 1):
        pairs = [(i, i ^ tables[parity(i & mix)][step]) for i in range(n_all)]
        if step == 0:
            twice = lax.optimization_barrier(jnp.concatenate([held, held], axis=0))
            held = twice.at[rows:].set(lax.ppermute(held, AXES, pairs))
        else:
            held = jnp.concatenate([held, lax.ppermute(held, AXES, pairs)], axis=0)
    other = lax.ppermute(held, "shard", [(0, 1), (1, 0)])
    half = held.shape[0]
    spare = 8 if half * 2 <= BLOCK else 2 * half
    out = pl.pallas_call(
        functools.partial(label_kernel, rows, n_blk),
        out_shape=jax.ShapeDtypeStruct(cand_ids.shape[::-1], jnp.float32),
        in_specs=[pl.BlockSpec(memory_space=pltpu.VMEM)] * 4,
        out_specs=pl.BlockSpec(memory_space=pltpu.VMEM),
        scratch_shapes=[pltpu.VMEM((spare, queries.shape[0]), jnp.float32)],
        compiler_params=pltpu.CompilerParams(vmem_limit_bytes=40 * 2**20),
    )(queries, held, other, cand_ids.T)
    return out.T


def solution(mesh):
    return jax.shard_map(
        body,
        mesh=mesh,
        in_specs=(
            P(("groups", "blk"), None),
            P(("groups", "blk", "shard"), None),
            P(("groups", "blk"), None),
        ),
        out_specs=P(("groups", "blk"), None),
        check_vma=False,
    )
```

time: 131 us -> 17.6 us (0.13)
  local copies, waits for them, and re-layouts: 78.2 us -> 1.14 us
  blocking collectives: 38.1 us -> 0 us
  matrix products: 10.9 us -> 0 us
  starting transfers between devices: 0 us -> 7.59 us
  waiting for transfers between devices: 0 us -> 6.23 us
  other arithmetic: 2.53 us -> 0.83 us
  Pallas kernels: 0 us -> 1.54 us
    gather x16 -> x0, local copies, waits for them, and re-layouts: 63.9 us -> none  [one_group(): chosen = jnp.take(corpus_rows, jnp.clip(ids, 0, height - 1), axis=0)]
    all_gather x4 -> x0, blocking collectives: 38.1 us -> none  [the longest x1 32.6 us: body(): corpus_rows = lax.all_gather(passages, 'blk', axis=0, tiled=True)]
    squeeze x16 -> x0, local copies, waits for them, and re-layouts: 12.9 us -> none  [pick_rows(): lax.map(one_group, (qgroups, igroups)).reshape(total, where_ids.shape[1])]
    dot_general x17 -> x0, matrix products: 10.9 us -> none  [the longest x16 9.34 us: one_group(): jnp.einsum('qd,qkd->qk', block, chosen, preferred_element_type=jnp.float32)]
    ppermute x0 -> x4, starting transfers between devices: none -> 7.59 us  [the longest x2 3.55 us: body(): held = jnp.concatenate([held, lax.ppermute(held, AXES, pairs)], axis=0)]
    ppermute x0 -> x4, waiting for transfers between devices: none -> 6.23 us  [the longest x2 4.16 us: body(): held = jnp.concatenate([held, lax.ppermute(held, AXES, pairs)], axis=0)]
    pallas_call x0 -> x1, Pallas kernels: none -> 1.54 us  [body(): pl.pallas_call(functools.partial(label_kernel, rows, n_blk), out_shape=ja...]
  transfers between devices with their start and end apart: 0 -> 4, of which waited for: 0 -> 4; matrix products, arithmetic and copies ran while one was open for 0% -> 5% of each run, Pallas kernels for 0% -> 0%
where the time goes in v1:
time: 17.6 us; the launch traced here: 17.4 us
  starting transfers between devices  7.59 us (43%)
  waiting for transfers between devices  6.23 us (35%)
  Pallas kernels  1.54 us (9%)
  local copies, waits for them, and re-layouts  1.14 us (6%)
  other arithmetic  0.83 us (5%)
    ppermute x2, waiting for transfers between devices, body(): held = jnp.concatenate([held, lax.ppermute(held, AXES, pairs)], axis=0)  4.16 us
    ppermute x2, starting transfers between devices, body(): held = jnp.concatenate([held, lax.ppermute(held, AXES, pairs)], axis=0)  3.55 us
    ppermute x1, starting transfers between devices, body(): held = twice.at[rows:].set(lax.ppermute(held, AXES, pairs))  3.48 us
    pallas_call x1, Pallas kernels, body(): pl.pallas_call(functools.partial(label_kernel, rows, n_blk), out_shape=ja...  1.54 us
    unnamed x4, local copies, waits for them, and re-layouts  1.14 us
    ppermute x1, waiting for transfers between devices, body(): other = lax.ppermute(held, 'shard', [(0, 1), (1, 0)])  1.07 us
    ppermute x1, waiting for transfers between devices, body(): held = twice.at[rows:].set(lax.ppermute(held, AXES, pairs))  1.01 us
    concatenate x1, other arithmetic, body(): twice = lax.optimization_barrier(jnp.concatenate([held, held], axis=0))  0.81 us
  transfers between devices with their start and end apart: 4, of which 4 were waited for; matrix products, arithmetic and copies ran while one was open for 5% of the time, Pallas kernels for 0%

profile of v1, /device:TPU:0, one launch (start us, length us, event | category | flops | bytes accessed | tf_op | source)
XLA Modules:
  0.0 17.4 jit_solution(2926357757197785736)
XLA Ops:
  0.0 3.5 %collective-permute-start = (bf16[16,768]{1,0:T(8,128)(2,1)}, bf16[16,768]{1,0:T(8,128)(2,1)S(1)}, u32[]{:S(2)}, u32[]{:S(2)}) collective-permute-start(bf16[16,768]{1,0:T(8,128)(2,1)} %param.6), channel_id=1, source_target_pairs={{0,9},{1,8},{2,11},{3,10},{4,13},{5,12},{6,15},{7,14},{8,1},{9,0},... | collective-permute-start | bytes 73736 | tf_op jit(solution)/shard_map/ppermute | solution.py:133
  3.5 0.8 %pad_maximum_fusion.2 = bf16[32,768]{1,0:T(8,128)(2,1)S(1)} fusion(bf16[16,768]{1,0:T(8,128)(2,1)} %param.6), kind=kLoop, calls=%fused_computation.2 | loop fusion | flops 98304 | bytes 73728 | tf_op jit(solution)/shard_map/concatenate | solution.py:132
  4.3 1.0 %collective-permute-done = bf16[16,768]{1,0:T(8,128)(2,1)S(1)} collective-permute-done((bf16[16,768]{1,0:T(8,128)(2,1)}, bf16[16,768]{1,0:T(8,128)(2,1)S(1)}, u32[]{:S(2)}, u32[]{:S(2)}) %collective-permute-start) | collective-permute-done | bytes 24608 | tf_op jit(solution)/shard_map/ppermute | solution.py:133
  5.3 1.8 %collective-permute-start.1 = (bf16[32,768]{1,0:T(8,128)(2,1)S(1)}, bf16[32,768]{1,0:T(8,128)(2,1)S(1)}, u32[]{:S(2)}, u32[]{:S(2)}) collective-permute-start(bf16[32,768]{1,0:T(8,128)(2,1)S(1)} %constant_dynamic-update-slice_fusion), channel_id=1, source_target_pairs={{0,5},{1,2},{2,1},{3,6},{4,7},{5,0},{6,3},{7,4},{8,13},{9,10},{10,... | collective-permute-start | bytes 147464 | tf_op jit(solution)/shard_map/ppermute | solution.py:135
  7.1 1.8 %collective-permute-done.1 = bf16[32,768]{1,0:T(8,128)(2,1)S(1)} collective-permute-done((bf16[32,768]{1,0:T(8,128)(2,1)S(1)}, bf16[32,768]{1,0:T(8,128)(2,1)S(1)}, u32[]{:S(2)}, u32[]{:S(2)}) %collective-permute-start.1) | collective-permute-done | bytes 49184 | tf_op jit(solution)/shard_map/ppermute | solution.py:135
  8.9 0.0 copy-start.1
  8.9 1.7 %collective-permute-start.2 = (bf16[64,768]{1,0:T(8,128)(2,1)S(1)}, bf16[64,768]{1,0:T(8,128)(2,1)S(1)}, u32[]{:S(2)}, u32[]{:S(2)}) collective-permute-start(bf16[64,768]{1,0:T(8,128)(2,1)S(1)} %pad_maximum_fusion.1), channel_id=1, source_target_pairs={{0,3},{1,4},{2,7},{3,0},{4,1},{5,6},{6,5},{7,2},{8,11},{9,12},{10,... | collective-permute-start | bytes 294920 | tf_op jit(solution)/shard_map/ppermute | solution.py:135
  10.6 2.4 %collective-permute-done.2 = bf16[64,768]{1,0:T(8,128)(2,1)S(1)} collective-permute-done((bf16[64,768]{1,0:T(8,128)(2,1)S(1)}, bf16[64,768]{1,0:T(8,128)(2,1)S(1)}, u32[]{:S(2)}, u32[]{:S(2)}) %collective-permute-start.2) | collective-permute-done | bytes 98336 | tf_op jit(solution)/shard_map/ppermute | solution.py:135
  13.0 0.6 %collective-permute-start.3 = (bf16[128,768]{1,0:T(8,128)(2,1)S(1)}, bf16[128,768]{1,0:T(8,128)(2,1)S(1)}, u32[]{:S(2)}, u32[]{:S(2)}) collective-permute-start(bf16[128,768]{1,0:T(8,128)(2,1)S(1)} %pad_maximum_fusion.own_ref), channel_id=1, source_target_pairs={{0,1},{1,0},{2,3},{3,2},{4,5},{5,4},{6,7},{7,6},{8,9},{9,8},{10,11... | collective-permute-start | bytes 589832 | tf_op jit(solution)/shard_map/ppermute | solution.py:136
  13.6 1.1 %collective-permute-done.3.other_ref = bf16[128,768]{1,0:T(8,128)(2,1)S(1)} collective-permute-done((bf16[128,768]{1,0:T(8,128)(2,1)S(1)}, bf16[128,768]{1,0:T(8,128)(2,1)S(1)}, u32[]{:S(2)}, u32[]{:S(2)}) %collective-permute-start.3) | collective-permute-done | bytes 196640 | tf_op jit(solution)/shard_map/ppermute | solution.py:136
  14.7 0.0 copy-done.1
  14.7 0.0 copy-start
  14.7 1.1 %copy-done = bf16[512,768]{1,0:T(8,128)(2,1)S(1)} copy-done((bf16[512,768]{1,0:T(8,128)(2,1)S(1)}, bf16[512,768]{1,0:T(8,128)(2,1)}, u32[]{:S(2)}) %copy-start) | copy-done | bytes 786456
  15.8 1.5 %shard_map.37 = f32[32,512]{1,0:T(8,128)} custom-call(bf16[512,768]{1,0:T(8,128)(2,1)S(1)} %copy-done, bf16[128,768]{1,0:T(8,128)(2,1)S(1)} %pad_maximum_fusion.own_ref, bf16[128,768]{1,0:T(8,128)(2,1)S(1)} %collective-permute-done.3.other_ref, s32[32,512]{1,0:T(8,128)S(1)} %bitcast.2), custom_call_target="tpu_custom_call" | custom-call | tf_op jit(solution)/shard_map/pallas_call | solution.py:139
  (3 shorter events, 0.0 us)
Async XLA Ops:
  0.0 5.3 %collective-permute-start = (bf16[16,768]{1,0:T(8,128)(2,1)}, bf16[16,768]{1,0:T(8,128)(2,1)S(1)}, u32[]{:S(2)}, u32[]{:S(2)}) collective-permute-start(bf16[16,768]{1,0:T(8,128)(2,1)} %param.6), channel_id=1, source_target_pairs={{0,9},{1,8},{2,11},{3,10},{4,13},{5,12},{6,15},{7,14},{8,1},{9,0},... | collective-permute-start | bytes 73736 | tf_op jit(solution)/shard_map/ppermute | solution.py:133
  5.3 3.6 %collective-permute-start.1 = (bf16[32,768]{1,0:T(8,128)(2,1)S(1)}, bf16[32,768]{1,0:T(8,128)(2,1)S(1)}, u32[]{:S(2)}, u32[]{:S(2)}) collective-permute-start(bf16[32,768]{1,0:T(8,128)(2,1)S(1)} %constant_dynamic-update-slice_fusion), channel_id=1, source_target_pairs={{0,5},{1,2},{2,1},{3,6},{4,7},{5,0},{6,3},{7,4},{8,13},{9,10},{10,... | collective-permute-start | bytes 147464 | tf_op jit(solution)/shard_map/ppermute | solution.py:135
  8.9 5.8 %copy-start.1 = (s32[512,32]{0,1:T(8,128)S(1)}, s32[512,32]{0,1:T(8,128)}, u32[]{:S(2)}) copy-start(s32[512,32]{0,1:T(8,128)} %param.7) | copy-start | bytes 196612
  8.9 4.1 %collective-permute-start.2 = (bf16[64,768]{1,0:T(8,128)(2,1)S(1)}, bf16[64,768]{1,0:T(8,128)(2,1)S(1)}, u32[]{:S(2)}, u32[]{:S(2)}) collective-permute-start(bf16[64,768]{1,0:T(8,128)(2,1)S(1)} %pad_maximum_fusion.1), channel_id=1, source_target_pairs={{0,3},{1,4},{2,7},{3,0},{4,1},{5,6},{6,5},{7,2},{8,11},{9,12},{10,... | collective-permute-start | bytes 294920 | tf_op jit(solution)/shard_map/ppermute | solution.py:135
  13.0 1.6 %collective-permute-start.3 = (bf16[128,768]{1,0:T(8,128)(2,1)S(1)}, bf16[128,768]{1,0:T(8,128)(2,1)S(1)}, u32[]{:S(2)}, u32[]{:S(2)}) collective-permute-start(bf16[128,768]{1,0:T(8,128)(2,1)S(1)} %pad_maximum_fusion.own_ref), channel_id=1, source_target_pairs={{0,1},{1,0},{2,3},{3,2},{4,5},{5,4},{6,7},{7,6},{8,9},{9,8},{10,11... | collective-permute-start | bytes 589832 | tf_op jit(solution)/shard_map/ppermute | solution.py:136
  14.7 1.1 %copy-start = (bf16[512,768]{1,0:T(8,128)(2,1)S(1)}, bf16[512,768]{1,0:T(8,128)(2,1)}, u32[]{:S(2)}) copy-start(bf16[512,768]{1,0:T(8,128)(2,1)} %q_ref.1) | copy-start | bytes 2359300

commit v2 on v0

v2 whole, which is shorter than its diff:
```python
import functools

import jax
import jax.numpy as jnp
from jax import lax
from jax.experimental import pallas as pl
from jax.experimental.pallas import tpu as pltpu
from jax.sharding import PartitionSpec as P

SCALE = 0.2
AXES = ("blk", "shard")
BLOCK = 256
VMEM = pl.BlockSpec(memory_space=pltpu.VMEM)


def parity(value):
    return value.bit_count() & 1


def doubling_masks(n_blk):
    return [(2 << bit) | 1 for bit in range(n_blk.bit_length() - 2, 1, -1)]


def direct_masks(kind):
    return (7, 5, 3) if kind else (7, 3, 5)


def local_ids(ids, rows, n_blk):
    me = lax.axis_index("blk") * 2 + lax.axis_index("shard")
    kind = (me ^ (me >> 1) ^ (me >> 2)) & 1
    shift = rows.bit_length() - 1
    source = (ids >> shift) ^ me
    one, two = (source >> 1) & 1, (source >> 2) & 1
    low = jnp.where(kind == 0, one, two)
    high = jnp.where(kind == 0, two, one)
    theirs = (source & 1) ^ (one | two)
    steps = doubling_masks(n_blk)
    place = ((low ^ high) << 1 | high) << len(steps)
    for step, mask in enumerate(steps):
        bit = (source >> (mask.bit_length() - 1)) & 1
        theirs = theirs ^ bit
        place = place | bit << step
    place = place | theirs << (len(steps) + 2)
    return (place << shift) | (ids & (rows - 1))


def absorb(state, logits, ids, start):
    top, total, picked = state
    new_top = jnp.maximum(top, jnp.max(logits, axis=0, keepdims=True))
    new_total = total * jnp.exp(top - new_top) + jnp.sum(
        jnp.exp(logits - new_top), axis=0, keepdims=True
    )
    chosen = []
    for k in range(0, ids.shape[0], 8):
        local = ids[k : k + 8] - start
        chunk, row = local >> 3, local & 7
        value = picked[k : k + 8]
        for c in range(logits.shape[0] // 8):
            found = jnp.take_along_axis(
                logits[c * 8 : c * 8 + 8], row, axis=0, mode="promise_in_bounds"
            )
            value = jnp.where(chunk == c, found, value)
        chosen.append(value)
    return (new_top, new_total, jnp.concatenate(chosen, axis=0))


def absorb_rows(state, refs, q_ref, ids, start):
    def one(state, rows, at):
        logits = SCALE * lax.dot_general(
            rows, q_ref[...], (((1,), (1,)), ((), ())), preferred_element_type=jnp.float32
        )
        return absorb(state, logits, ids, at)

    count = refs[0].shape[0]
    if count * len(refs) <= BLOCK:
        return one(state, jnp.concatenate([ref[...] for ref in refs], axis=0), start)

    for ref in refs:

        def step(index, state, ref=ref, start=start):
            at = pl.multiple_of(index * BLOCK, BLOCK)
            return one(state, ref[pl.ds(at, BLOCK)], start + at)

        state = lax.fori_loop(0, count // BLOCK, step, state)
        start = start + count
    return state


def empty(ids):
    wide = (1, ids.shape[1])
    return (
        jnp.full(wide, -jnp.inf, jnp.float32),
        jnp.zeros(wide, jnp.float32),
        jnp.zeros(ids.shape, jnp.float32),
    )


def first_kernel(rows, n_blk, q_ref, a_ref, b_ref, ids_ref, local_ref, top_ref, total_ref, picked_ref):
    local = local_ids(ids_ref[...], rows, n_blk)
    local_ref[...] = local
    state = absorb_rows(empty(local), (a_ref, b_ref), q_ref, local, 0)
    top_ref[...], total_ref[...], picked_ref[...] = state


def second_kernel(start, q_ref, a_ref, b_ref, local_ref, top_ref, total_ref, picked_ref, out_ref):
    state = (top_ref[...], total_ref[...], picked_ref[...])
    top, total, picked = absorb_rows(state, (a_ref, b_ref), q_ref, local_ref[...], start)
    count = picked.shape[0]
    out_ref[:count] = picked
    out_ref[count:] = jnp.broadcast_to(top + jnp.log(total), (8, picked.shape[1]))


def last_kernel(mine_ref, other_ref, out_ref):
    count = out_ref.shape[0]
    mine, other = mine_ref[count : count + 1], other_ref[count : count + 1]
    top = jnp.maximum(mine, other)
    normalizer = top + jnp.log(jnp.exp(mine - top) + jnp.exp(other - top))
    out_ref[...] = mine_ref[:count] + other_ref[:count] - normalizer


def cost(n_rows, queries, ids):
    return pl.CostEstimate(
        flops=2 * n_rows * queries.shape[0] * queries.shape[1],
        bytes_accessed=2 * (queries.size + n_rows * queries.shape[1]) + 8 * ids.size,
        transcendentals=n_rows * queries.shape[0],
    )


PARAMS = pltpu.CompilerParams(vmem_limit_bytes=40 * 2**20)


def first_call(rows, n_blk, queries, pieces, ids):
    wide = jax.ShapeDtypeStruct((1, ids.shape[1]), jnp.float32)
    return pl.pallas_call(
        functools.partial(first_kernel, rows, n_blk),
        out_shape=(
            jax.ShapeDtypeStruct(ids.shape, jnp.int32),
            wide,
            wide,
            jax.ShapeDtypeStruct(ids.shape, jnp.float32),
        ),
        in_specs=[VMEM] * 4,
        out_specs=(VMEM,) * 4,
        compiler_params=PARAMS,
        cost_estimate=cost(2 * pieces[0].shape[0], queries, ids),
    )(queries, *pieces, ids)


def second_call(queries, pieces, local, state):
    return pl.pallas_call(
        functools.partial(second_kernel, 2 * pieces[0].shape[0]),
        out_shape=jax.ShapeDtypeStruct((local.shape[0] + 8, local.shape[1]), jnp.float32),
        in_specs=[VMEM] * 7,
        out_specs=VMEM,
        compiler_params=PARAMS,
        cost_estimate=cost(2 * pieces[0].shape[0], queries, local),
    )(queries, *pieces, local, *state)


def last_call(mine, other, count):
    return pl.pallas_call(
        last_kernel,
        out_shape=jax.ShapeDtypeStruct((count, mine.shape[1]), jnp.float32),
        in_specs=[VMEM] * 2,
        out_specs=VMEM,
        compiler_params=PARAMS,
    )(mine, other)


def body(queries, passages, cand_ids):
    rows = passages.shape[0]
    n_blk = lax.axis_size("blk")
    n_all = 2 * n_blk
    direct = [direct_masks(i.bit_count() & 1) for i in range(8)]
    held = passages
    for step, mask in enumerate(doubling_masks(n_blk)):
        got = lax.ppermute(held, AXES, [(i, i ^ mask) for i in range(n_all)])
        if step == 0:
            twice = lax.optimization_barrier(jnp.concatenate([held, held], axis=0))
            held = twice.at[rows:].set(got)
        else:
            held = jnp.concatenate([held, got], axis=0)
    far, near, last = (
        lax.ppermute(held, AXES, [(i, i ^ direct[i % 8][turn]) for i in range(n_all)])
        for turn in range(3)
    )
    local, *state = first_call(rows, n_blk, queries, [held, far], cand_ids.T)
    mine = second_call(queries, [near, last], local, state)
    other = lax.ppermute(mine, "shard", [(0, 1), (1, 0)])
    return last_call(mine, other, cand_ids.shape[1]).T


def solution(mesh):
    return jax.shard_map(
        body,
        mesh=mesh,
        in_specs=(
            P(("groups", "blk"), None),
            P(("groups", "blk", "shard"), None),
            P(("groups", "blk"), None),
        ),
        out_specs=P(("groups", "blk"), None),
        check_vma=False,
    )
```

time: 131 us -> 15.3 us (0.12)
  local copies, waits for them, and re-layouts: 78.2 us -> 1.14 us
  blocking collectives: 38.1 us -> 0 us
  matrix products: 10.9 us -> 0 us
  starting transfers between devices: 0 us -> 7.05 us
  waiting for transfers between devices: 0 us -> 4.45 us
  other arithmetic: 2.53 us -> 0.81 us
  Pallas kernels: 0 us -> 1.59 us
    gather x16 -> x0, local copies, waits for them, and re-layouts: 63.9 us -> none  [one_group(): chosen = jnp.take(corpus_rows, jnp.clip(ids, 0, height - 1), axis=0)]
    all_gather x4 -> x0, blocking collectives: 38.1 us -> none  [the longest x1 32.6 us: body(): corpus_rows = lax.all_gather(passages, 'blk', axis=0, tiled=True)]
    squeeze x16 -> x0, local copies, waits for them, and re-layouts: 12.9 us -> none  [pick_rows(): lax.map(one_group, (qgroups, igroups)).reshape(total, where_ids.shape[1])]
    dot_general x17 -> x0, matrix products: 10.9 us -> none  [the longest x16 9.34 us: one_group(): jnp.einsum('qd,qkd->qk', block, chosen, preferred_element_type=jnp.float32)]
    ppermute x0 -> x5, starting transfers between devices: none -> 7.05 us  [the longest x1 3.48 us: body(): got = lax.ppermute(held, AXES, [(i, i ^ mask) for i in range(n_all)])]
    ppermute x0 -> x5, waiting for transfers between devices: none -> 4.45 us  [the longest x3 2.29 us: body(): lax.ppermute(held, AXES, [(i, i ^ direct[i % 8][turn]) for i in range(n_a...]
    pallas_call x0 -> x3, Pallas kernels: none -> 1.59 us  [the longest x1 0.66 us: last_call(): pl.pallas_call(last_kernel, out_shape=jax.ShapeDtypeStruct((count, mine.s...]
  transfers between devices with their start and end apart: 0 -> 5, of which waited for: 0 -> 4; matrix products, arithmetic and copies ran while one was open for 0% -> 5% of each run, Pallas kernels for 0% -> 3%
where the time goes in v2:
time: 15.3 us; the launch traced here: 15.1 us
  starting transfers between devices  7.05 us (46%)
  waiting for transfers between devices  4.45 us (29%)
  Pallas kernels  1.59 us (10%)
  local copies, waits for them, and re-layouts  1.14 us (7%)
  other arithmetic  0.81 us (5%)
    ppermute x1, starting transfers between devices, body(): got = lax.ppermute(held, AXES, [(i, i ^ mask) for i in range(n_all)])  3.48 us
    ppermute x3, starting transfers between devices, body(): lax.ppermute(held, AXES, [(i, i ^ direct[i % 8][turn]) for i in range(n_a...  3.39 us
    ppermute x3, waiting for transfers between devices, body(): lax.ppermute(held, AXES, [(i, i ^ direct[i % 8][turn]) for i in range(n_a...  2.29 us
    ppermute x1, waiting for transfers between devices, body(): other = lax.ppermute(mine, 'shard', [(0, 1), (1, 0)])  1.16 us
    unnamed x4, local copies, waits for them, and re-layouts  1.14 us
    ppermute x1, waiting for transfers between devices, body(): got = lax.ppermute(held, AXES, [(i, i ^ mask) for i in range(n_all)])  1.01 us
    concatenate x1, other arithmetic, body(): twice = lax.optimization_barrier(jnp.concatenate([held, held], axis=0))  0.81 us
    pallas_call x1, Pallas kernels, last_call(): pl.pallas_call(last_kernel, out_shape=jax.ShapeDtypeStruct((count, mine.s...  0.66 us
  transfers between devices with their start and end apart: 5, of which 4 were waited for; matrix products, arithmetic and copies ran while one was open for 5% of the time, Pallas kernels for 3%

profile of v2, /device:TPU:0, one launch (start us, length us, event | category | flops | bytes accessed | tf_op | source)
XLA Modules:
  0.0 15.1 jit_solution(9634235924295161338)
XLA Ops:
  0.0 0.0 copy-start.1
  0.0 3.5 %collective-permute-start = (bf16[16,768]{1,0:T(8,128)(2,1)}, bf16[16,768]{1,0:T(8,128)(2,1)S(1)}, u32[]{:S(2)}, u32[]{:S(2)}) collective-permute-start(bf16[16,768]{1,0:T(8,128)(2,1)} %param.6), channel_id=1, source_target_pairs={{0,9},{1,8},{2,11},{3,10},{4,13},{5,12},{6,15},{7,14},{8,1},{9,0},... | collective-permute-start | bytes 73736 | tf_op jit(solution)/shard_map/ppermute | solution.py:177
  3.5 0.8 %pad_maximum_fusion = bf16[32,768]{1,0:T(8,128)(2,1)S(1)} fusion(bf16[16,768]{1,0:T(8,128)(2,1)} %param.6), kind=kLoop, calls=%fused_computation | loop fusion | flops 98304 | bytes 73728 | tf_op jit(solution)/shard_map/concatenate | solution.py:179
  4.3 1.0 %collective-permute-done = bf16[16,768]{1,0:T(8,128)(2,1)S(1)} collective-permute-done((bf16[16,768]{1,0:T(8,128)(2,1)}, bf16[16,768]{1,0:T(8,128)(2,1)S(1)}, u32[]{:S(2)}, u32[]{:S(2)}) %collective-permute-start) | collective-permute-done | bytes 24608 | tf_op jit(solution)/shard_map/ppermute | solution.py:177
  5.3 2.8 %collective-permute-start.3 = (bf16[32,768]{1,0:T(8,128)(2,1)S(1)}, bf16[32,768]{1,0:T(8,128)(2,1)S(1)}, u32[]{:S(2)}, u32[]{:S(2)}) collective-permute-start(bf16[32,768]{1,0:T(8,128)(2,1)S(1)} %constant_dynamic-update-slice_fusion.a_ref), channel_id=1, source_target_pairs={{0,7},{1,6},{2,5},{3,4},{4,3},{5,2},{6,1},{7,0},{8,15},{9,14},{10,... | collective-permute-start | bytes 147464 | tf_op jit(solution)/shard_map/ppermute | solution.py:184
  8.1 0.5 %collective-permute-start.1 = (bf16[32,768]{1,0:T(8,128)(2,1)S(1)}, bf16[32,768]{1,0:T(8,128)(2,1)S(1)}, u32[]{:S(2)}, u32[]{:S(2)}) collective-permute-start(bf16[32,768]{1,0:T(8,128)(2,1)S(1)} %constant_dynamic-update-slice_fusion.a_ref), channel_id=1, source_target_pairs={{0,3},{1,4},{2,7},{3,0},{4,1},{5,6},{6,5},{7,2},{8,11},{9,12},{10,... | collective-permute-start | bytes 147464 | tf_op jit(solution)/shard_map/ppermute | solution.py:184
  8.6 0.1 collective-permute-start.2
  8.7 1.5 %collective-permute-done.3.b_ref = bf16[32,768]{1,0:T(8,128)(2,1)S(1)} collective-permute-done((bf16[32,768]{1,0:T(8,128)(2,1)S(1)}, bf16[32,768]{1,0:T(8,128)(2,1)S(1)}, u32[]{:S(2)}, u32[]{:S(2)}) %collective-permute-start.3) | collective-permute-done | bytes 49184 | tf_op jit(solution)/shard_map/ppermute | solution.py:184
  10.2 0.0 copy-done.1
  10.2 0.0 copy-start
  10.2 1.1 %copy-done = bf16[512,768]{1,0:T(8,128)(2,1)S(1)} copy-done((bf16[512,768]{1,0:T(8,128)(2,1)S(1)}, bf16[512,768]{1,0:T(8,128)(2,1)}, u32[]{:S(2)}) %copy-start) | copy-done | bytes 786456
  11.3 0.5 %shard_map.37 = (s32[32,512]{1,0:T(8,128)S(1)}, f32[1,512]{1,0:T(1,128)S(1)}, f32[1,512]{1,0:T(1,128)S(1)}, f32[32,512]{1,0:T(8,128)S(1)}) custom-call(bf16[512,768]{1,0:T(8,128)(2,1)S(1)} %copy-done, bf16[32,768]{1,0:T(8,128)(2,1)S(1)} %constant_dynamic-update-slice_fusion.a_ref, bf16[32,768]{1,0:T(8,128)(2,1)S(1)} %collective-permute-done.3.b_ref, ...), custom_call_target="tpu_custom_call" | custom-call | flops 50331648 | bytes 1015808 | tf_op jit(solution)/shard_map/pallas_call | solution.py:134
  11.8 0.0 collective-permute-done.1.a_ref
  11.8 0.8 %collective-permute-done.2.b_ref = bf16[32,768]{1,0:T(8,128)(2,1)S(1)} collective-permute-done((bf16[32,768]{1,0:T(8,128)(2,1)S(1)}, bf16[32,768]{1,0:T(8,128)(2,1)S(1)}, u32[]{:S(2)}, u32[]{:S(2)}) %collective-permute-start.2) | collective-permute-done | bytes 49184 | tf_op jit(solution)/shard_map/ppermute | solution.py:184
  12.6 0.5 %shard_map.38.mine_ref = f32[40,512]{1,0:T(8,128)S(1)} custom-call(bf16[512,768]{1,0:T(8,128)(2,1)S(1)} %copy-done, bf16[32,768]{1,0:T(8,128)(2,1)S(1)} %collective-permute-done.1.a_ref, bf16[32,768]{1,0:T(8,128)(2,1)S(1)} %collective-permute-done.2.b_ref, s32[32,512]{1,0:T(8,128)S(1)} %get-tuple-element.21.local_ref, ...), custom_call_target="tpu_custom_call" | custom-call | flops 50331648 | bytes 1015808 | tf_op jit(solution)/shard_map/pallas_call | solution.py:150
  13.1 0.2 %collective-permute-start.4 = (f32[40,512]{1,0:T(8,128)S(1)}, f32[40,512]{1,0:T(8,128)S(1)}, u32[]{:S(2)}, u32[]{:S(2)}) collective-permute-start(f32[40,512]{1,0:T(8,128)S(1)} %shard_map.38.mine_ref), channel_id=1, source_target_pairs={{0,1},{1,0},{2,3},{3,2},{4,5},{5,4},{6,7},{7,6},{8,9},{9,8},{10,11... | collective-permute-start | bytes 245768 | tf_op jit(solution)/shard_map/ppermute | solution.py:189
  13.2 1.2 %collective-permute-done.4.other_ref = f32[40,512]{1,0:T(8,128)S(1)} collective-permute-done((f32[40,512]{1,0:T(8,128)S(1)}, f32[40,512]{1,0:T(8,128)S(1)}, u32[]{:S(2)}, u32[]{:S(2)}) %collective-permute-start.4) | collective-permute-done | bytes 81952 | tf_op jit(solution)/shard_map/ppermute | solution.py:189
  14.4 0.7 %shard_map.39 = f32[32,512]{1,0:T(8,128)} custom-call(f32[40,512]{1,0:T(8,128)S(1)} %shard_map.38.mine_ref, f32[40,512]{1,0:T(8,128)S(1)} %collective-permute-done.4.other_ref), custom_call_target="tpu_custom_call" | custom-call | tf_op jit(solution)/shard_map/pallas_call | solution.py:161
  (1 shorter events, 0.0 us)
Async XLA Ops:
  0.0 10.2 %copy-start.1 = (s32[512,32]{0,1:T(8,128)S(1)}, s32[512,32]{0,1:T(8,128)}, u32[]{:S(2)}) copy-start(s32[512,32]{0,1:T(8,128)} %param.7) | copy-start | bytes 196612
  0.0 5.3 %collective-permute-start = (bf16[16,768]{1,0:T(8,128)(2,1)}, bf16[16,768]{1,0:T(8,128)(2,1)S(1)}, u32[]{:S(2)}, u32[]{:S(2)}) collective-permute-start(bf16[16,768]{1,0:T(8,128)(2,1)} %param.6), channel_id=1, source_target_pairs={{0,9},{1,8},{2,11},{3,10},{4,13},{5,12},{6,15},{7,14},{8,1},{9,0},... | collective-permute-start | bytes 73736 | tf_op jit(solution)/shard_map/ppermute | solution.py:177
  5.3 4.9 %collective-permute-start.3 = (bf16[32,768]{1,0:T(8,128)(2,1)S(1)}, bf16[32,768]{1,0:T(8,128)(2,1)S(1)}, u32[]{:S(2)}, u32[]{:S(2)}) collective-permute-start(bf16[32,768]{1,0:T(8,128)(2,1)S(1)} %constant_dynamic-update-slice_fusion.a_ref), channel_id=1, source_target_pairs={{0,7},{1,6},{2,5},{3,4},{4,3},{5,2},{6,1},{7,0},{8,15},{9,14},{10,... | collective-permute-start | bytes 147464 | tf_op jit(solution)/shard_map/ppermute | solution.py:184
  8.1 3.7 %collective-permute-start.1 = (bf16[32,768]{1,0:T(8,128)(2,1)S(1)}, bf16[32,768]{1,0:T(8,128)(2,1)S(1)}, u32[]{:S(2)}, u32[]{:S(2)}) collective-permute-start(bf16[32,768]{1,0:T(8,128)(2,1)S(1)} %constant_dynamic-update-slice_fusion.a_ref), channel_id=1, source_target_pairs={{0,3},{1,4},{2,7},{3,0},{4,1},{5,6},{6,5},{7,2},{8,11},{9,12},{10,... | collective-permute-start | bytes 147464 | tf_op jit(solution)/shard_map/ppermute | solution.py:184
  8.6 4.0 %collective-permute-start.2 = (bf16[32,768]{1,0:T(8,128)(2,1)S(1)}, bf16[32,768]{1,0:T(8,128)(2,1)S(1)}, u32[]{:S(2)}, u32[]{:S(2)}) collective-permute-start(bf16[32,768]{1,0:T(8,128)(2,1)S(1)} %constant_dynamic-update-slice_fusion.a_ref), channel_id=1, source_target_pairs={{0,5},{1,2},{2,1},{3,6},{4,7},{5,0},{6,3},{7,4},{8,13},{9,10},{10,... | collective-permute-start | bytes 147464 | tf_op jit(solution)/shard_map/ppermute | solution.py:184
  10.2 1.1 %copy-start = (bf16[512,768]{1,0:T(8,128)(2,1)S(1)}, bf16[512,768]{1,0:T(8,128)(2,1)}, u32[]{:S(2)}) copy-start(bf16[512,768]{1,0:T(8,128)(2,1)} %q_ref.3) | copy-start | bytes 2359300
  13.1 1.3 %collective-permute-start.4 = (f32[40,512]{1,0:T(8,128)S(1)}, f32[40,512]{1,0:T(8,128)S(1)}, u32[]{:S(2)}, u32[]{:S(2)}) collective-permute-start(f32[40,512]{1,0:T(8,128)S(1)} %shard_map.38.mine_ref), channel_id=1, source_target_pairs={{0,1},{1,0},{2,3},{3,2},{4,5},{5,4},{6,7},{7,6},{8,9},{9,8},{10,11... | collective-permute-start | bytes 245768 | tf_op jit(solution)/shard_map/ppermute | solution.py:189

commit v3 on v2

--- a/solution.py
+++ b/solution.py
@@ -17,28 +17,66 @@
     return value.bit_count() & 1
 
 
+CROSSED = 0
+MASKS = (3, 4, 7)
+ORDERS = (
+    (2, 1, 0),
+    (0, 2, 1),
+    (2, 0, 1),
+    (2, 1, 0),
+    (2, 1, 0),
+    (0, 2, 1),
+    (2, 0, 1),
+    (2, 1, 0),
+    (2, 1, 0),
+    (0, 2, 1),
+    (2, 0, 1),
+    (2, 1, 0),
+    (2, 1, 0),
+    (0, 2, 1),
+    (2, 0, 1),
+    (2, 1, 0),
+)
+
+
 def doubling_masks(n_blk):
-    return [(2 << bit) | 1 for bit in range(n_blk.bit_length() - 2, 1, -1)]
-
-
-def direct_masks(kind):
-    return (7, 5, 3) if kind else (7, 3, 5)
+    return [(2 << bit) | CROSSED for bit in range(n_blk.bit_length() - 2, 1, -1)]
+
+
+def target(number, turn):
+    return number ^ MASKS[ORDERS[number & 15][turn]]
+
+
+def turns_of(which):
+    code = 0
+    for number in range(16):
+        source = number ^ MASKS[which]
+        code |= ORDERS[source].index(which) << (2 * number)
+    return code
 
 
 def local_ids(ids, rows, n_blk):
     me = lax.axis_index("blk") * 2 + lax.axis_index("shard")
-    kind = (me ^ (me >> 1) ^ (me >> 2)) & 1
     shift = rows.bit_length() - 1
     source = (ids >> shift) ^ me
     one, two = (source >> 1) & 1, (source >> 2) & 1
-    low = jnp.where(kind == 0, one, two)
-    high = jnp.where(kind == 0, two, one)
-    theirs = (source & 1) ^ (one | two)
+    at = (me & 7) << 1
+    low_half = ((me >> 3) & 1) == 0
+
+    def slot_of(which):
+        code = turns_of(which)
+        low, high = code & 0xFFFF, code >> 16
+        return 1 + ((jnp.where(low_half, low, high) >> at) & 3)
+
+    slots = [slot_of(which) for which in range(3)]
+    slot = jnp.where(two == 0, one * slots[0], jnp.where(one == 0, slots[1], slots[2]))
+    core = [mask & 1 for mask in MASKS]
+    theirs = (source & 1) ^ jnp.where(two == 0, one * core[0], jnp.where(one == 0, core[1], core[2]))
     steps = doubling_masks(n_blk)
-    place = ((low ^ high) << 1 | high) << len(steps)
+    place = slot << len(steps)
     for step, mask in enumerate(steps):
         bit = (source >> (mask.bit_length() - 1)) & 1
-        theirs = theirs ^ bit
+        theirs = theirs ^ (bit * CROSSED)
         place = place | bit << step
     place = place | theirs << (len(steps) + 2)
     return (place << shift) | (ids & (rows - 1))
@@ -95,19 +133,24 @@
     )
 
 
-def first_kernel(rows, n_blk, q_ref, a_ref, b_ref, ids_ref, local_ref, top_ref, total_ref, picked_ref):
+def first_kernel(rows, n_blk, q_ref, held_ref, ids_ref, local_ref, top_ref, total_ref, picked_ref):
     local = local_ids(ids_ref[...], rows, n_blk)
     local_ref[...] = local
-    state = absorb_rows(empty(local), (a_ref, b_ref), q_ref, local, 0)
+    state = absorb_rows(empty(local), (held_ref,), q_ref, local, 0)
     top_ref[...], total_ref[...], picked_ref[...] = state
 
 
-def second_kernel(start, q_ref, a_ref, b_ref, local_ref, top_ref, total_ref, picked_ref, out_ref):
+def next_kernel(start, n_pieces, q_ref, local_ref, top_ref, total_ref, picked_ref, *refs):
+    pieces, outs = refs[:n_pieces], refs[n_pieces:]
     state = (top_ref[...], total_ref[...], picked_ref[...])
-    top, total, picked = absorb_rows(state, (a_ref, b_ref), q_ref, local_ref[...], start)
+    state = absorb_rows(state, pieces, q_ref, local_ref[...], start)
+    if len(outs) == 3:
+        outs[0][...], outs[1][...], outs[2][...] = state
+        return
+    top, total, picked = state
     count = picked.shape[0]
-    out_ref[:count] = picked
-    out_ref[count:] = jnp.broadcast_to(top + jnp.log(total), (8, picked.shape[1]))
+    outs[0][:count] = picked
+    outs[0][count:] = jnp.broadcast_to(top + jnp.log(total), (8, picked.shape[1]))
 
 
 def last_kernel(mine_ref, other_ref, out_ref):
@@ -129,32 +172,33 @@
 PARAMS = pltpu.CompilerParams(vmem_limit_bytes=40 * 2**20)
 
 
-def first_call(rows, n_blk, queries, pieces, ids):
+def state_shapes(ids):
     wide = jax.ShapeDtypeStruct((1, ids.shape[1]), jnp.float32)
+    return (wide, wide, jax.ShapeDtypeStruct(ids.shape, jnp.float32))
+
+
+def first_call(rows, n_blk, queries, held, ids):
     return pl.pallas_call(
         functools.partial(first_kernel, rows, n_blk),
-        out_shape=(
-            jax.ShapeDtypeStruct(ids.shape, jnp.int32),
-            wide,
-            wide,
-            jax.ShapeDtypeStruct(ids.shape, jnp.float32),
-        ),
-        in_specs=[VMEM] * 4,
+        out_shape=(jax.ShapeDtypeStruct(ids.shape, jnp.int32), *state_shapes(ids)),
+        in_specs=[VMEM] * 3,
         out_specs=(VMEM,) * 4,
         compiler_params=PARAMS,
-        cost_estimate=cost(2 * pieces[0].shape[0], queries, ids),
-    )(queries, *pieces, ids)
-
-
-def second_call(queries, pieces, local, state):
+        cost_estimate=cost(held.shape[0], queries, ids),
+    )(queries, held, ids)
+
+
+def next_call(queries, pieces, start, local, state, last):
+    part = jax.ShapeDtypeStruct((local.shape[0] + 8, local.shape[1]), jnp.float32)
+    shapes = (part,) if last else state_shapes(local)
     return pl.pallas_call(
-        functools.partial(second_kernel, 2 * pieces[0].shape[0]),
-        out_shape=jax.ShapeDtypeStruct((local.shape[0] + 8, local.shape[1]), jnp.float32),
-        in_specs=[VMEM] * 7,
-        out_specs=VMEM,
+        functools.partial(next_kernel, start, len(pieces)),
+        out_shape=shapes,
+        in_specs=[VMEM] * (5 + len(pieces)),
+        out_specs=(VMEM,) * len(shapes),
         compiler_params=PARAMS,
-        cost_estimate=cost(2 * pieces[0].shape[0], queries, local),
-    )(queries, *pieces, local, *state)
+        cost_estimate=cost(len(pieces) * pieces[0].shape[0], queries, local),
+    )(queries, local, *state, *pieces)
 
 
 def last_call(mine, other, count):
@@ -171,7 +215,6 @@
     rows = passages.shape[0]
     n_blk = lax.axis_size("blk")
     n_all = 2 * n_blk
-    direct = [direct_masks(i.bit_count() & 1) for i in range(8)]
     held = passages
     for step, mask in enumerate(doubling_masks(n_blk)):
         got = lax.ppermute(held, AXES, [(i, i ^ mask) for i in range(n_all)])
@@ -181,11 +224,13 @@
         else:
             held = jnp.concatenate([held, got], axis=0)
     far, near, last = (
-        lax.ppermute(held, AXES, [(i, i ^ direct[i % 8][turn]) for i in range(n_all)])
+        lax.ppermute(held, AXES, [(i, target(i, turn)) for i in range(n_all)])
         for turn in range(3)
     )
-    local, *state = first_call(rows, n_blk, queries, [held, far], cand_ids.T)
-    mine = second_call(queries, [near, last], local, state)
+    count = held.shape[0]
+    local, *state = first_call(rows, n_blk, queries, held, cand_ids.T)
+    state = next_call(queries, [far], count, local, state, False)
+    (mine,) = next_call(queries, [near, last], 2 * count, local, state, True)
     other = lax.ppermute(mine, "shard", [(0, 1), (1, 0)])
     return last_call(mine, other, cand_ids.shape[1]).T
 

time: 15.3 us -> 14.5 us (0.948)
  waiting for transfers between devices: 4.45 us -> 2.94 us
  Pallas kernels: 1.59 us -> 1.94 us
  starting transfers between devices: 7.05 us -> 7.38 us
    ppermute x3, waiting for transfers between devices: 2.29 us -> 0.65 us  [body(): lax.ppermute(held, AXES, [(i, target(i, turn)) for i in range(n_all)])]
    ppermute x1, starting transfers between devices: 3.48 us -> 4.04 us  [body(): got = lax.ppermute(held, AXES, [(i, i ^ mask) for i in range(n_all)])]
    pallas_call x1 -> x2, Pallas kernels: 0.47 us -> 0.88 us  [next_call(): pl.pallas_call(functools.partial(next_kernel, start, len(pieces)), out_sh...]
    ppermute x3, starting transfers between devices: 3.39 us -> 3.08 us  [body(): lax.ppermute(held, AXES, [(i, target(i, turn)) for i in range(n_all)])]
    ppermute x1, waiting for transfers between devices: 1.01 us -> 1.21 us  [body(): got = lax.ppermute(held, AXES, [(i, i ^ mask) for i in range(n_all)])]
  transfers between devices with their start and end apart: 5 -> 5, of which waited for: 4 -> 4; matrix products, arithmetic and copies ran while one was open for 5% -> 6% of each run, Pallas kernels for 3% -> 6%
where the time goes in v3:
time: 14.5 us; the launch traced here: 14.2 us
  starting transfers between devices  7.38 us (51%)
  waiting for transfers between devices  2.94 us (20%)
  Pallas kernels  1.94 us (13%)
  local copies, waits for them, and re-layouts  1.14 us (8%)
  other arithmetic  0.81 us (6%)
    ppermute x1, starting transfers between devices, body(): got = lax.ppermute(held, AXES, [(i, i ^ mask) for i in range(n_all)])  4.04 us
    ppermute x3, starting transfers between devices, body(): lax.ppermute(held, AXES, [(i, target(i, turn)) for i in range(n_all)])  3.08 us
    ppermute x1, waiting for transfers between devices, body(): got = lax.ppermute(held, AXES, [(i, i ^ mask) for i in range(n_all)])  1.21 us
    unnamed x4, local copies, waits for them, and re-layouts  1.14 us
    ppermute x1, waiting for transfers between devices, body(): other = lax.ppermute(mine, 'shard', [(0, 1), (1, 0)])  1.08 us
    pallas_call x2, Pallas kernels, next_call(): pl.pallas_call(functools.partial(next_kernel, start, len(pieces)), out_sh...  0.88 us
    concatenate x1, other arithmetic, body(): twice = lax.optimization_barrier(jnp.concatenate([held, held], axis=0))  0.81 us
    pallas_call x1, Pallas kernels, last_call(): pl.pallas_call(last_kernel, out_shape=jax.ShapeDtypeStruct((count, mine.s...  0.66 us
  transfers between devices with their start and end apart: 5, of which 4 were waited for; matrix products, arithmetic and copies ran while one was open for 6% of the time, Pallas kernels for 6%

profile of v3, /device:TPU:0, one launch (start us, length us, event | category | flops | bytes accessed | tf_op | source)
XLA Modules:
  0.0 14.2 jit_solution(5161505260630135194)
XLA Ops:
  0.0 0.0 copy-start.1
  0.0 4.0 %collective-permute-start = (bf16[16,768]{1,0:T(8,128)(2,1)}, bf16[16,768]{1,0:T(8,128)(2,1)S(1)}, u32[]{:S(2)}, u32[]{:S(2)}) collective-permute-start(bf16[16,768]{1,0:T(8,128)(2,1)} %param.6), channel_id=1, source_target_pairs={{0,8},{1,9},{2,10},{3,11},{4,12},{5,13},{6,14},{7,15},{8,0},{9,1},... | collective-permute-start | bytes 73736 | tf_op jit(solution)/shard_map/ppermute | solution.py:220
  4.0 0.8 %pad_maximum_fusion = bf16[32,768]{1,0:T(8,128)(2,1)S(1)} fusion(bf16[16,768]{1,0:T(8,128)(2,1)} %param.6), kind=kLoop, calls=%fused_computation | loop fusion | flops 98304 | bytes 73728 | tf_op jit(solution)/shard_map/concatenate | solution.py:222
  4.8 1.2 %collective-permute-done = bf16[16,768]{1,0:T(8,128)(2,1)S(1)} collective-permute-done((bf16[16,768]{1,0:T(8,128)(2,1)}, bf16[16,768]{1,0:T(8,128)(2,1)S(1)}, u32[]{:S(2)}, u32[]{:S(2)}) %collective-permute-start) | collective-permute-done | bytes 24608 | tf_op jit(solution)/shard_map/ppermute | solution.py:220
  6.1 1.1 %collective-permute-start.1 = (bf16[32,768]{1,0:T(8,128)(2,1)S(1)}, bf16[32,768]{1,0:T(8,128)(2,1)S(1)}, u32[]{:S(2)}, u32[]{:S(2)}) collective-permute-start(bf16[32,768]{1,0:T(8,128)(2,1)S(1)} %constant_dynamic-update-slice_fusion.held_ref), channel_id=1, source_target_pairs={{0,7},{1,2},{2,5},{3,4},{4,3},{5,6},{6,1},{7,0},{8,15},{9,10},{10,... | collective-permute-start | bytes 147464 | tf_op jit(solution)/shard_map/ppermute | solution.py:227
  7.2 0.8 %collective-permute-start.2 = (bf16[32,768]{1,0:T(8,128)(2,1)S(1)}, bf16[32,768]{1,0:T(8,128)(2,1)S(1)}, u32[]{:S(2)}, u32[]{:S(2)}) collective-permute-start(bf16[32,768]{1,0:T(8,128)(2,1)S(1)} %constant_dynamic-update-slice_fusion.held_ref), channel_id=1, source_target_pairs={{0,4},{1,6},{2,1},{3,7},{4,0},{5,2},{6,5},{7,3},{8,12},{9,14},{10,... | collective-permute-start | bytes 147464 | tf_op jit(solution)/shard_map/ppermute | solution.py:227
  8.0 1.2 %collective-permute-start.3 = (bf16[32,768]{1,0:T(8,128)(2,1)S(1)}, bf16[32,768]{1,0:T(8,128)(2,1)S(1)}, u32[]{:S(2)}, u32[]{:S(2)}) collective-permute-start(bf16[32,768]{1,0:T(8,128)(2,1)S(1)} %constant_dynamic-update-slice_fusion.held_ref), channel_id=1, source_target_pairs={{0,3},{1,5},{2,6},{3,0},{4,7},{5,1},{6,2},{7,4},{8,11},{9,13},{10,... | collective-permute-start | bytes 147464 | tf_op jit(solution)/shard_map/ppermute | solution.py:227
  9.2 0.0 copy-done.1
  9.2 0.0 copy-start
  9.2 1.1 %copy-done = bf16[512,768]{1,0:T(8,128)(2,1)S(1)} copy-done((bf16[512,768]{1,0:T(8,128)(2,1)S(1)}, bf16[512,768]{1,0:T(8,128)(2,1)}, u32[]{:S(2)}) %copy-start) | copy-done | bytes 786456
  10.3 0.4 %shard_map.37 = (s32[32,512]{1,0:T(8,128)S(1)}, f32[1,512]{1,0:T(1,128)S(1)}, f32[1,512]{1,0:T(1,128)S(1)}, f32[32,512]{1,0:T(8,128)S(1)}) custom-call(bf16[512,768]{1,0:T(8,128)(2,1)S(1)} %copy-done, bf16[32,768]{1,0:T(8,128)(2,1)S(1)} %constant_dynamic-update-slice_fusion.held_ref, s32[32,512]{1,0:T(8,128)S(1)} %bitcast.2), custom_call_target="tpu_custom_call" | custom-call | flops 25165824 | bytes 966656 | tf_op jit(solution)/shard_map/pallas_call | solution.py:181
  10.7 0.0 collective-permute-done.1.refs_0_
  10.7 0.4 %shard_map.38 = (f32[1,512]{1,0:T(1,128)S(1)}, f32[1,512]{1,0:T(1,128)S(1)}, f32[32,512]{1,0:T(8,128)S(1)}) custom-call(bf16[512,768]{1,0:T(8,128)(2,1)S(1)} %copy-done, s32[32,512]{1,0:T(8,128)S(1)} %get-tuple-element.24.local_ref, f32[1,512]{1,0:T(1,128)S(1)} %get-tuple-element.25.top_ref, f32[1,512]{1,0:T(1,128)S(1)} %get-tuple-element.26.total_ref, ...), custom_call_target="tpu_custom_call" | custom-call | flops 25165824 | bytes 966656 | tf_op jit(solution)/shard_map/pallas_call | solution.py:194
  11.1 0.4 %collective-permute-done.2.refs_0_ = bf16[32,768]{1,0:T(8,128)(2,1)S(1)} collective-permute-done((bf16[32,768]{1,0:T(8,128)(2,1)S(1)}, bf16[32,768]{1,0:T(8,128)(2,1)S(1)}, u32[]{:S(2)}, u32[]{:S(2)}) %collective-permute-start.2) | collective-permute-done | bytes 49184 | tf_op jit(solution)/shard_map/ppermute | solution.py:227
  11.5 0.3 %collective-permute-done.3.refs_1_ = bf16[32,768]{1,0:T(8,128)(2,1)S(1)} collective-permute-done((bf16[32,768]{1,0:T(8,128)(2,1)S(1)}, bf16[32,768]{1,0:T(8,128)(2,1)S(1)}, u32[]{:S(2)}, u32[]{:S(2)}) %collective-permute-start.3) | collective-permute-done | bytes 49184 | tf_op jit(solution)/shard_map/ppermute | solution.py:227
  11.8 0.5 %shard_map.39.mine_ref = f32[40,512]{1,0:T(8,128)S(1)} custom-call(bf16[512,768]{1,0:T(8,128)(2,1)S(1)} %copy-done, s32[32,512]{1,0:T(8,128)S(1)} %get-tuple-element.24.local_ref, f32[1,512]{1,0:T(1,128)S(1)} %get-tuple-element.28.top_ref, f32[1,512]{1,0:T(1,128)S(1)} %get-tuple-element.29.total_ref, f32[32,512]{1,0:T(8,128)S(1)} %get-tuple-element.30.picked_ref, ...), custom_call_target="tpu_custom_call" | custom-call | flops 50331648 | bytes 1015808 | tf_op jit(solution)/shard_map/pallas_call | solution.py:194
  12.2 0.3 %collective-permute-start.4 = (f32[40,512]{1,0:T(8,128)S(1)}, f32[40,512]{1,0:T(8,128)S(1)}, u32[]{:S(2)}, u32[]{:S(2)}) collective-permute-start(f32[40,512]{1,0:T(8,128)S(1)} %shard_map.39.mine_ref), channel_id=1, source_target_pairs={{0,1},{1,0},{2,3},{3,2},{4,5},{5,4},{6,7},{7,6},{8,9},{9,8},{10,11... | collective-permute-start | bytes 245768 | tf_op jit(solution)/shard_map/ppermute | solution.py:234
  12.5 1.1 %collective-permute-done.4.other_ref = f32[40,512]{1,0:T(8,128)S(1)} collective-permute-done((f32[40,512]{1,0:T(8,128)S(1)}, f32[40,512]{1,0:T(8,128)S(1)}, u32[]{:S(2)}, u32[]{:S(2)}) %collective-permute-start.4) | collective-permute-done | bytes 81952 | tf_op jit(solution)/shard_map/ppermute | solution.py:234
  13.6 0.7 %shard_map.40 = f32[32,512]{1,0:T(8,128)} custom-call(f32[40,512]{1,0:T(8,128)S(1)} %shard_map.39.mine_ref, f32[40,512]{1,0:T(8,128)S(1)} %collective-permute-done.4.other_ref), custom_call_target="tpu_custom_call" | custom-call | tf_op jit(solution)/shard_map/pallas_call | solution.py:205
  (1 shorter events, 0.0 us)
Async XLA Ops:
  0.0 9.2 %copy-start.1 = (s32[512,32]{0,1:T(8,128)S(1)}, s32[512,32]{0,1:T(8,128)}, u32[]{:S(2)}) copy-start(s32[512,32]{0,1:T(8,128)} %param.7) | copy-start | bytes 196612
  0.0 6.1 %collective-permute-start = (bf16[16,768]{1,0:T(8,128)(2,1)}, bf16[16,768]{1,0:T(8,128)(2,1)S(1)}, u32[]{:S(2)}, u32[]{:S(2)}) collective-permute-start(bf16[16,768]{1,0:T(8,128)(2,1)} %param.6), channel_id=1, source_target_pairs={{0,8},{1,9},{2,10},{3,11},{4,12},{5,13},{6,14},{7,15},{8,0},{9,1},... | collective-permute-start | bytes 73736 | tf_op jit(solution)/shard_map/ppermute | solution.py:220
  6.1 4.6 %collective-permute-start.1 = (bf16[32,768]{1,0:T(8,128)(2,1)S(1)}, bf16[32,768]{1,0:T(8,128)(2,1)S(1)}, u32[]{:S(2)}, u32[]{:S(2)}) collective-permute-start(bf16[32,768]{1,0:T(8,128)(2,1)S(1)} %constant_dynamic-update-slice_fusion.held_ref), channel_id=1, source_target_pairs={{0,7},{1,2},{2,5},{3,4},{4,3},{5,6},{6,1},{7,0},{8,15},{9,10},{10,... | collective-permute-start | bytes 147464 | tf_op jit(solution)/shard_map/ppermute | solution.py:227
  7.2 4.3 %collective-permute-start.2 = (bf16[32,768]{1,0:T(8,128)(2,1)S(1)}, bf16[32,768]{1,0:T(8,128)(2,1)S(1)}, u32[]{:S(2)}, u32[]{:S(2)}) collective-permute-start(bf16[32,768]{1,0:T(8,128)(2,1)S(1)} %constant_dynamic-update-slice_fusion.held_ref), channel_id=1, source_target_pairs={{0,4},{1,6},{2,1},{3,7},{4,0},{5,2},{6,5},{7,3},{8,12},{9,14},{10,... | collective-permute-start | bytes 147464 | tf_op jit(solution)/shard_map/ppermute | solution.py:227
  8.0 3.8 %collective-permute-start.3 = (bf16[32,768]{1,0:T(8,128)(2,1)S(1)}, bf16[32,768]{1,0:T(8,128)(2,1)S(1)}, u32[]{:S(2)}, u32[]{:S(2)}) collective-permute-start(bf16[32,768]{1,0:T(8,128)(2,1)S(1)} %constant_dynamic-update-slice_fusion.held_ref), channel_id=1, source_target_pairs={{0,3},{1,5},{2,6},{3,0},{4,7},{5,1},{6,2},{7,4},{8,11},{9,13},{10,... | collective-permute-start | bytes 147464 | tf_op jit(solution)/shard_map/ppermute | solution.py:227
  9.2 1.1 %copy-start = (bf16[512,768]{1,0:T(8,128)(2,1)S(1)}, bf16[512,768]{1,0:T(8,128)(2,1)}, u32[]{:S(2)}) copy-start(bf16[512,768]{1,0:T(8,128)(2,1)} %q_ref.5) | copy-start | bytes 2359300
  12.2 1.3 %collective-permute-start.4 = (f32[40,512]{1,0:T(8,128)S(1)}, f32[40,512]{1,0:T(8,128)S(1)}, u32[]{:S(2)}, u32[]{:S(2)}) collective-permute-start(f32[40,512]{1,0:T(8,128)S(1)} %shard_map.39.mine_ref), channel_id=1, source_target_pairs={{0,1},{1,0},{2,3},{3,2},{4,5},{5,4},{6,7},{7,6},{8,9},{9,8},{10,11... | collective-permute-start | bytes 245768 | tf_op jit(solution)/shard_map/ppermute | solution.py:234

commit v4 on v3

--- a/solution.py
+++ b/solution.py
@@ -17,30 +17,34 @@
     return value.bit_count() & 1
 
 
-CROSSED = 0
-MASKS = (3, 4, 7)
+CROSSED = 0b11
+MASKS = (2, 5, 7)
 ORDERS = (
-    (2, 1, 0),
-    (0, 2, 1),
-    (2, 0, 1),
-    (2, 1, 0),
-    (2, 1, 0),
-    (0, 2, 1),
-    (2, 0, 1),
-    (2, 1, 0),
-    (2, 1, 0),
-    (0, 2, 1),
-    (2, 0, 1),
-    (2, 1, 0),
-    (2, 1, 0),
-    (0, 2, 1),
-    (2, 0, 1),
-    (2, 1, 0),
+    (0, 2, 1),
+    (1, 2, 0),
+    (0, 2, 1),
+    (1, 2, 0),
+    (2, 1, 0),
+    (0, 2, 1),
+    (2, 1, 0),
+    (0, 2, 1),
+    (0, 2, 1),
+    (1, 2, 0),
+    (0, 2, 1),
+    (1, 2, 0),
+    (2, 1, 0),
+    (0, 2, 1),
+    (2, 1, 0),
+    (0, 2, 1),
 )
 
 
-def doubling_masks(n_blk):
-    return [(2 << bit) | CROSSED for bit in range(n_blk.bit_length() - 2, 1, -1)]
+def doubling_bits(n_blk):
+    return [2 << bit for bit in range(n_blk.bit_length() - 2, 1, -1)]
+
+
+def crosses(number):
+    return (CROSSED >> ((number >> 1) & 3)) & 1
 
 
 def target(number, turn):
@@ -72,11 +76,12 @@
     slot = jnp.where(two == 0, one * slots[0], jnp.where(one == 0, slots[1], slots[2]))
     core = [mask & 1 for mask in MASKS]
     theirs = (source & 1) ^ jnp.where(two == 0, one * core[0], jnp.where(one == 0, core[1], core[2]))
-    steps = doubling_masks(n_blk)
+    steps = doubling_bits(n_blk)
     place = slot << len(steps)
+    cross = crosses(ids >> shift)
     for step, mask in enumerate(steps):
         bit = (source >> (mask.bit_length() - 1)) & 1
-        theirs = theirs ^ (bit * CROSSED)
+        theirs = theirs ^ (bit & cross)
         place = place | bit << step
     place = place | theirs << (len(steps) + 2)
     return (place << shift) | (ids & (rows - 1))
@@ -105,7 +110,7 @@
 def absorb_rows(state, refs, q_ref, ids, start):
     def one(state, rows, at):
         logits = SCALE * lax.dot_general(
-            rows, q_ref[...], (((1,), (1,)), ((), ())), preferred_element_type=jnp.float32
+            rows, q_ref[...], (((1,), (0,)), ((), ())), preferred_element_type=jnp.float32
         )
         return absorb(state, logits, ids, at)
 
@@ -163,9 +168,9 @@
 
 def cost(n_rows, queries, ids):
     return pl.CostEstimate(
-        flops=2 * n_rows * queries.shape[0] * queries.shape[1],
-        bytes_accessed=2 * (queries.size + n_rows * queries.shape[1]) + 8 * ids.size,
-        transcendentals=n_rows * queries.shape[0],
+        flops=2 * n_rows * queries.size,
+        bytes_accessed=2 * (queries.size + n_rows * queries.shape[0]) + 8 * ids.size,
+        transcendentals=n_rows * queries.shape[1],
     )
 
 
@@ -215,9 +220,10 @@
     rows = passages.shape[0]
     n_blk = lax.axis_size("blk")
     n_all = 2 * n_blk
+    queries = lax.optimization_barrier(queries.T)
     held = passages
-    for step, mask in enumerate(doubling_masks(n_blk)):
-        got = lax.ppermute(held, AXES, [(i, i ^ mask) for i in range(n_all)])
+    for step, mask in enumerate(doubling_bits(n_blk)):
+        got = lax.ppermute(held, AXES, [(i, i ^ mask ^ crosses(i)) for i in range(n_all)])
         if step == 0:
             twice = lax.optimization_barrier(jnp.concatenate([held, held], axis=0))
             held = twice.at[rows:].set(got)

time: 14.5 us -> 14.3 us (0.986)
  Pallas kernels: 1.94 us -> 1.64 us
  local copies, waits for them, and re-layouts: 1.14 us -> 1.42 us
  starting transfers between devices: 7.38 us -> 7.14 us
    ppermute x1, starting transfers between devices: 4.04 us -> 3.48 us  [body(): lax.ppermute(held, AXES, [(i, i ^ mask ^ crosses(i)) for i in range(n_all)])]
    ppermute x3, waiting for transfers between devices: 0.65 us -> 1.13 us  [body(): lax.ppermute(held, AXES, [(i, target(i, turn)) for i in range(n_all)])]
    unnamed x4 -> x3, local copies, waits for them, and re-layouts: 1.14 us -> 1.41 us
    ppermute x1, waiting for transfers between devices: 1.21 us -> 1.01 us  [body(): lax.ppermute(held, AXES, [(i, i ^ mask ^ crosses(i)) for i in range(n_all)])]
    pallas_call x2, Pallas kernels: 0.88 us -> 0.68 us  [next_call(): pl.pallas_call(functools.partial(next_kernel, start, len(pieces)), out_sh...]
    ppermute x3, starting transfers between devices: 3.08 us -> 3.26 us  [body(): lax.ppermute(held, AXES, [(i, target(i, turn)) for i in range(n_all)])]
  transfers between devices with their start and end apart: 5 -> 5, of which waited for: 4 -> 3; matrix products, arithmetic and copies ran while one was open for 6% -> 16% of each run, Pallas kernels for 6% -> 4%
where the time goes in v4:
time: 14.3 us; the launch traced here: 14.1 us
  starting transfers between devices  7.14 us (50%)
  waiting for transfers between devices  3.07 us (21%)
  Pallas kernels  1.64 us (11%)
  local copies, waits for them, and re-layouts  1.42 us (10%)
  other arithmetic  0.81 us (6%)
    ppermute x1, starting transfers between devices, body(): lax.ppermute(held, AXES, [(i, i ^ mask ^ crosses(i)) for i in range(n_all)])  3.48 us
    ppermute x3, starting transfers between devices, body(): lax.ppermute(held, AXES, [(i, target(i, turn)) for i in range(n_all)])  3.26 us
    unnamed x3, local copies, waits for them, and re-layouts  1.41 us
    ppermute x3, waiting for transfers between devices, body(): lax.ppermute(held, AXES, [(i, target(i, turn)) for i in range(n_all)])  1.13 us
    ppermute x1, waiting for transfers between devices, body(): lax.ppermute(held, AXES, [(i, i ^ mask ^ crosses(i)) for i in range(n_all)])  1.01 us
    ppermute x1, waiting for transfers between devices, body(): other = lax.ppermute(mine, 'shard', [(0, 1), (1, 0)])  0.94 us
    concatenate x1, other arithmetic, body(): twice = lax.optimization_barrier(jnp.concatenate([held, held], axis=0))  0.81 us
    pallas_call x2, Pallas kernels, next_call(): pl.pallas_call(functools.partial(next_kernel, start, len(pieces)), out_sh...  0.68 us
  transfers between devices with their start and end apart: 5, of which 3 were waited for; matrix products, arithmetic and copies ran while one was open for 16% of the time, Pallas kernels for 4%

profile of v4, /device:TPU:0, one launch (start us, length us, event | category | flops | bytes accessed | tf_op | source)
XLA Modules:
  0.0 14.1 jit_solution(831610792679310960)
XLA Ops:
  0.0 3.5 %collective-permute-start = (bf16[16,768]{1,0:T(8,128)(2,1)}, bf16[16,768]{1,0:T(8,128)(2,1)S(1)}, u32[]{:S(2)}, u32[]{:S(2)}) collective-permute-start(bf16[16,768]{1,0:T(8,128)(2,1)} %param.6), channel_id=1, source_target_pairs={{0,9},{1,8},{2,11},{3,10},{4,12},{5,13},{6,14},{7,15},{8,1},{9,0},... | collective-permute-start | bytes 73736 | tf_op jit(solution)/shard_map/ppermute | solution.py:226
  3.5 0.8 %pad_maximum_fusion = bf16[32,768]{1,0:T(8,128)(2,1)S(1)} fusion(bf16[16,768]{1,0:T(8,128)(2,1)} %param.6), kind=kLoop, calls=%fused_computation | loop fusion | flops 98304 | bytes 73728 | tf_op jit(solution)/shard_map/concatenate | solution.py:228
  4.3 1.0 %collective-permute-done = bf16[16,768]{1,0:T(8,128)(2,1)S(1)} collective-permute-done((bf16[16,768]{1,0:T(8,128)(2,1)}, bf16[16,768]{1,0:T(8,128)(2,1)S(1)}, u32[]{:S(2)}, u32[]{:S(2)}) %collective-permute-start) | collective-permute-done | bytes 24608 | tf_op jit(solution)/shard_map/ppermute | solution.py:226
  5.3 0.0 copy-start
  5.3 2.0 %collective-permute-start.1 = (bf16[32,768]{1,0:T(8,128)(2,1)S(1)}, bf16[32,768]{1,0:T(8,128)(2,1)S(1)}, u32[]{:S(2)}, u32[]{:S(2)}) collective-permute-start(bf16[32,768]{1,0:T(8,128)(2,1)S(1)} %constant_dynamic-update-slice_fusion.held_ref), channel_id=1, source_target_pairs={{0,2},{1,4},{2,0},{3,6},{4,3},{5,7},{6,1},{7,5},{8,10},{9,12},{10,... | collective-permute-start | bytes 147464 | tf_op jit(solution)/shard_map/ppermute | solution.py:233
  7.3 0.2 %collective-permute-start.2 = (bf16[32,768]{1,0:T(8,128)(2,1)S(1)}, bf16[32,768]{1,0:T(8,128)(2,1)S(1)}, u32[]{:S(2)}, u32[]{:S(2)}) collective-permute-start(bf16[32,768]{1,0:T(8,128)(2,1)S(1)} %constant_dynamic-update-slice_fusion.held_ref), channel_id=1, source_target_pairs={{0,7},{1,6},{2,5},{3,4},{4,1},{5,2},{6,3},{7,0},{8,15},{9,14},{10,... | collective-permute-start | bytes 147464 | tf_op jit(solution)/shard_map/ppermute | solution.py:233
  7.5 1.1 %collective-permute-start.3 = (bf16[32,768]{1,0:T(8,128)(2,1)S(1)}, bf16[32,768]{1,0:T(8,128)(2,1)S(1)}, u32[]{:S(2)}, u32[]{:S(2)}) collective-permute-start(bf16[32,768]{1,0:T(8,128)(2,1)S(1)} %constant_dynamic-update-slice_fusion.held_ref), channel_id=1, source_target_pairs={{0,5},{1,3},{2,7},{3,1},{4,6},{5,0},{6,4},{7,2},{8,13},{9,11},{10,... | collective-permute-start | bytes 147464 | tf_op jit(solution)/shard_map/ppermute | solution.py:233
  8.6 1.4 %copy.4 = bf16[512,768]{0,1:T(8,128)(2,1)S(1)} copy(bf16[512,768]{1,0:T(8,128)(2,1)} %param.5) | data formatting | bytes 1572864 | tf_op args[0]
  10.0 0.0 copy-done
  10.0 0.3 %shard_map.37 = (s32[32,512]{1,0:T(8,128)S(1)}, f32[1,512]{1,0:T(1,128)S(1)}, f32[1,512]{1,0:T(1,128)S(1)}, f32[32,512]{1,0:T(8,128)S(1)}) custom-call(bf16[768,512]{1,0:T(8,128)(2,1)S(1)} %bitcast.3, bf16[32,768]{1,0:T(8,128)(2,1)S(1)} %constant_dynamic-update-slice_fusion.held_ref, s32[32,512]{1,0:T(8,128)S(1)} %bitcast.6), custom_call_target="tpu_custom_call" | custom-call | flops 25165824 | bytes 966656 | tf_op jit(solution)/shard_map/pallas_call | solution.py:186
  10.3 0.0 collective-permute-done.1.refs_0_
  10.3 0.3 %shard_map.38 = (f32[1,512]{1,0:T(1,128)S(1)}, f32[1,512]{1,0:T(1,128)S(1)}, f32[32,512]{1,0:T(8,128)S(1)}) custom-call(bf16[768,512]{1,0:T(8,128)(2,1)S(1)} %bitcast.4, s32[32,512]{1,0:T(8,128)S(1)} %get-tuple-element.24.local_ref, f32[1,512]{1,0:T(1,128)S(1)} %get-tuple-element.25.top_ref, f32[1,512]{1,0:T(1,128)S(1)} %get-tuple-element.26.total_ref, ...), custom_call_target="tpu_custom_call" | custom-call | flops 25165824 | bytes 966656 | tf_op jit(solution)/shard_map/pallas_call | solution.py:199
  10.6 1.1 %collective-permute-done.2.refs_0_ = bf16[32,768]{1,0:T(8,128)(2,1)S(1)} collective-permute-done((bf16[32,768]{1,0:T(8,128)(2,1)S(1)}, bf16[32,768]{1,0:T(8,128)(2,1)S(1)}, u32[]{:S(2)}, u32[]{:S(2)}) %collective-permute-start.2) | collective-permute-done | bytes 49184 | tf_op jit(solution)/shard_map/ppermute | solution.py:233
  11.7 0.0 collective-permute-done.3.refs_1_
  11.7 0.4 %shard_map.39.mine_ref = f32[40,512]{1,0:T(8,128)S(1)} custom-call(bf16[768,512]{1,0:T(8,128)(2,1)S(1)} %bitcast.5, s32[32,512]{1,0:T(8,128)S(1)} %get-tuple-element.24.local_ref, f32[1,512]{1,0:T(1,128)S(1)} %get-tuple-element.28.top_ref, f32[1,512]{1,0:T(1,128)S(1)} %get-tuple-element.29.total_ref, f32[32,512]{1,0:T(8,128)S(1)} %get-tuple-element.30.picked_ref, ...), custom_call_target="tpu_custom_call" | custom-call | flops 50331648 | bytes 1015808 | tf_op jit(solution)/shard_map/pallas_call | solution.py:199
  12.1 0.4 %collective-permute-start.4 = (f32[40,512]{1,0:T(8,128)S(1)}, f32[40,512]{1,0:T(8,128)S(1)}, u32[]{:S(2)}, u32[]{:S(2)}) collective-permute-start(f32[40,512]{1,0:T(8,128)S(1)} %shard_map.39.mine_ref), channel_id=1, source_target_pairs={{0,1},{1,0},{2,3},{3,2},{4,5},{5,4},{6,7},{7,6},{8,9},{9,8},{10,11... | collective-permute-start | bytes 245768 | tf_op jit(solution)/shard_map/ppermute | solution.py:240
  12.5 0.9 %collective-permute-done.4.other_ref = f32[40,512]{1,0:T(8,128)S(1)} collective-permute-done((f32[40,512]{1,0:T(8,128)S(1)}, f32[40,512]{1,0:T(8,128)S(1)}, u32[]{:S(2)}, u32[]{:S(2)}) %collective-permute-start.4) | collective-permute-done | bytes 81952 | tf_op jit(solution)/shard_map/ppermute | solution.py:240
  13.5 0.7 %shard_map.40 = f32[32,512]{1,0:T(8,128)} custom-call(f32[40,512]{1,0:T(8,128)S(1)} %shard_map.39.mine_ref, f32[40,512]{1,0:T(8,128)S(1)} %collective-permute-done.4.other_ref), custom_call_target="tpu_custom_call" | custom-call | tf_op jit(solution)/shard_map/pallas_call | solution.py:210
  (1 shorter events, 0.0 us)
Async XLA Ops:
  0.0 5.3 %collective-permute-start = (bf16[16,768]{1,0:T(8,128)(2,1)}, bf16[16,768]{1,0:T(8,128)(2,1)S(1)}, u32[]{:S(2)}, u32[]{:S(2)}) collective-permute-start(bf16[16,768]{1,0:T(8,128)(2,1)} %param.6), channel_id=1, source_target_pairs={{0,9},{1,8},{2,11},{3,10},{4,12},{5,13},{6,14},{7,15},{8,1},{9,0},... | collective-permute-start | bytes 73736 | tf_op jit(solution)/shard_map/ppermute | solution.py:226
  5.3 4.7 %copy-start = (s32[512,32]{0,1:T(8,128)S(1)}, s32[512,32]{0,1:T(8,128)}, u32[]{:S(2)}) copy-start(s32[512,32]{0,1:T(8,128)} %param.7) | copy-start | bytes 196612
  5.3 5.0 %collective-permute-start.1 = (bf16[32,768]{1,0:T(8,128)(2,1)S(1)}, bf16[32,768]{1,0:T(8,128)(2,1)S(1)}, u32[]{:S(2)}, u32[]{:S(2)}) collective-permute-start(bf16[32,768]{1,0:T(8,128)(2,1)S(1)} %constant_dynamic-update-slice_fusion.held_ref), channel_id=1, source_target_pairs={{0,2},{1,4},{2,0},{3,6},{4,3},{5,7},{6,1},{7,5},{8,10},{9,12},{10,... | collective-permute-start | bytes 147464 | tf_op jit(solution)/shard_map/ppermute | solution.py:233
  7.3 4.4 %collective-permute-start.2 = (bf16[32,768]{1,0:T(8,128)(2,1)S(1)}, bf16[32,768]{1,0:T(8,128)(2,1)S(1)}, u32[]{:S(2)}, u32[]{:S(2)}) collective-permute-start(bf16[32,768]{1,0:T(8,128)(2,1)S(1)} %constant_dynamic-update-slice_fusion.held_ref), channel_id=1, source_target_pairs={{0,7},{1,6},{2,5},{3,4},{4,1},{5,2},{6,3},{7,0},{8,15},{9,14},{10,... | collective-permute-start | bytes 147464 | tf_op jit(solution)/shard_map/ppermute | solution.py:233
  7.5 4.3 %collective-permute-start.3 = (bf16[32,768]{1,0:T(8,128)(2,1)S(1)}, bf16[32,768]{1,0:T(8,128)(2,1)S(1)}, u32[]{:S(2)}, u32[]{:S(2)}) collective-permute-start(bf16[32,768]{1,0:T(8,128)(2,1)S(1)} %constant_dynamic-update-slice_fusion.held_ref), channel_id=1, source_target_pairs={{0,5},{1,3},{2,7},{3,1},{4,6},{5,0},{6,4},{7,2},{8,13},{9,11},{10,... | collective-permute-start | bytes 147464 | tf_op jit(solution)/shard_map/ppermute | solution.py:233
  12.1 1.3 %collective-permute-start.4 = (f32[40,512]{1,0:T(8,128)S(1)}, f32[40,512]{1,0:T(8,128)S(1)}, u32[]{:S(2)}, u32[]{:S(2)}) collective-permute-start(f32[40,512]{1,0:T(8,128)S(1)} %shard_map.39.mine_ref), channel_id=1, source_target_pairs={{0,1},{1,0},{2,3},{3,2},{4,5},{5,4},{6,7},{7,6},{8,9},{9,8},{10,11... | collective-permute-start | bytes 245768 | tf_op jit(solution)/shard_map/ppermute | solution.py:240

commit v5 on v4

--- a/solution.py
+++ b/solution.py
@@ -17,25 +17,24 @@
     return value.bit_count() & 1
 
 
-CROSSED = 0b11
-MASKS = (2, 5, 7)
-ORDERS = (
-    (0, 2, 1),
-    (1, 2, 0),
-    (0, 2, 1),
-    (1, 2, 0),
-    (2, 1, 0),
-    (0, 2, 1),
-    (2, 1, 0),
-    (0, 2, 1),
-    (0, 2, 1),
-    (1, 2, 0),
-    (0, 2, 1),
-    (1, 2, 0),
-    (2, 1, 0),
-    (0, 2, 1),
-    (2, 1, 0),
-    (0, 2, 1),
+CROSSED = 0b10
+SENDS = (
+    (7, 2, 5),
+    (5, 7, 2),
+    (7, 2, 5),
+    (5, 7, 2),
+    (7, 5, 2),
+    (7, 2, 5),
+    (7, 5, 2),
+    (7, 2, 5),
+    (7, 2, 5),
+    (5, 7, 2),
+    (7, 2, 5),
+    (5, 7, 2),
+    (7, 5, 2),
+    (7, 2, 5),
+    (7, 5, 2),
+    (7, 2, 5),
 )
 
 
@@ -48,15 +47,18 @@
 
 
 def target(number, turn):
-    return number ^ MASKS[ORDERS[number & 15][turn]]
-
-
-def turns_of(which):
-    code = 0
+    return number ^ SENDS[number & 15][turn]
+
+
+def receives(which):
+    turns = cores = 0
     for number in range(16):
-        source = number ^ MASKS[which]
-        code |= ORDERS[source].index(which) << (2 * number)
-    return code
+        for source in (number ^ (which << 1), number ^ (which << 1) ^ 1):
+            for turn in range(3):
+                if target(source, turn) == number:
+                    turns |= turn << (2 * number)
+                    cores |= ((source ^ number) & 1) << number
+    return turns, cores
 
 
 def local_ids(ids, rows, n_blk):
@@ -64,18 +66,20 @@
     shift = rows.bit_length() - 1
     source = (ids >> shift) ^ me
     one, two = (source >> 1) & 1, (source >> 2) & 1
-    at = (me & 7) << 1
-    low_half = ((me >> 3) & 1) == 0
-
-    def slot_of(which):
-        code = turns_of(which)
-        low, high = code & 0xFFFF, code >> 16
-        return 1 + ((jnp.where(low_half, low, high) >> at) & 3)
-
-    slots = [slot_of(which) for which in range(3)]
-    slot = jnp.where(two == 0, one * slots[0], jnp.where(one == 0, slots[1], slots[2]))
-    core = [mask & 1 for mask in MASKS]
-    theirs = (source & 1) ^ jnp.where(two == 0, one * core[0], jnp.where(one == 0, core[1], core[2]))
+    here = me & 15
+
+    def of_this(which):
+        turns, cores = receives(which)
+        turn = jnp.where(here < 8, turns & 0xFFFF, turns >> 16) >> ((here & 7) << 1)
+        return 1 + (turn & 3), (cores >> here) & 1
+
+    (slot_1, core_1), (slot_2, core_2), (slot_3, core_3) = [of_this(which) for which in (1, 2, 3)]
+
+    def choose(own, first, second, third):
+        return jnp.where(two == 0, jnp.where(one == 0, own, first), jnp.where(one == 0, second, third))
+
+    slot = choose(0, slot_1, slot_2, slot_3)
+    theirs = (source & 1) ^ choose(0, core_1, core_2, core_3)
     steps = doubling_bits(n_blk)
     place = slot << len(steps)
     cross = crosses(ids >> shift)

time: 14.3 us -> 14.2 us (level)
  waiting for transfers between devices: 3.07 us -> 2.62 us
  starting transfers between devices: 7.14 us -> 7.5 us
    ppermute x3, waiting for transfers between devices: 1.13 us -> 0.48 us  [body(): lax.ppermute(held, AXES, [(i, target(i, turn)) for i in range(n_all)])]
    ppermute x1, starting transfers between devices: 3.48 us -> 4.04 us  [body(): lax.ppermute(held, AXES, [(i, i ^ mask ^ crosses(i)) for i in range(n_all)])]
    ppermute x3, starting transfers between devices: 3.26 us -> 2.93 us  [body(): lax.ppermute(held, AXES, [(i, target(i, turn)) for i in range(n_all)])]
    ppermute x1, waiting for transfers between devices: 1.01 us -> 1.21 us  [body(): lax.ppermute(held, AXES, [(i, i ^ mask ^ crosses(i)) for i in range(n_all)])]
where the time goes in v5:
time: 14.2 us; the launch traced here: 14 us
  starting transfers between devices  7.5 us (53%)
  waiting for transfers between devices  2.62 us (18%)
  Pallas kernels  1.64 us (12%)
  local copies, waits for them, and re-layouts  1.42 us (10%)
  other arithmetic  0.81 us (6%)
    ppermute x1, starting transfers between devices, body(): lax.ppermute(held, AXES, [(i, i ^ mask ^ crosses(i)) for i in range(n_all)])  4.04 us
    ppermute x3, starting transfers between devices, body(): lax.ppermute(held, AXES, [(i, target(i, turn)) for i in range(n_all)])  2.93 us
    unnamed x3, local copies, waits for them, and re-layouts  1.41 us
    ppermute x1, waiting for transfers between devices, body(): lax.ppermute(held, AXES, [(i, i ^ mask ^ crosses(i)) for i in range(n_all)])  1.21 us
    ppermute x1, waiting for transfers between devices, body(): other = lax.ppermute(mine, 'shard', [(0, 1), (1, 0)])  0.92 us
    concatenate x1, other arithmetic, body(): twice = lax.optimization_barrier(jnp.concatenate([held, held], axis=0))  0.81 us
    pallas_call x2, Pallas kernels, next_call(): pl.pallas_call(functools.partial(next_kernel, start, len(pieces)), out_sh...  0.68 us
    pallas_call x1, Pallas kernels, last_call(): pl.pallas_call(last_kernel, out_shape=jax.ShapeDtypeStruct((count, mine.s...  0.65 us
  transfers between devices with their start and end apart: 5, of which 3 were waited for; matrix products, arithmetic and copies ran while one was open for 16% of the time, Pallas kernels for 4%

profile of v5, /device:TPU:0, one launch (start us, length us, event | category | flops | bytes accessed | tf_op | source)
XLA Modules:
  0.0 14.0 jit_solution(16551008819271165914)
XLA Ops:
  0.0 4.0 %collective-permute-start = (bf16[16,768]{1,0:T(8,128)(2,1)}, bf16[16,768]{1,0:T(8,128)(2,1)S(1)}, u32[]{:S(2)}, u32[]{:S(2)}) collective-permute-start(bf16[16,768]{1,0:T(8,128)(2,1)} %param.6), channel_id=1, source_target_pairs={{0,8},{1,9},{2,11},{3,10},{4,12},{5,13},{6,14},{7,15},{8,0},{9,1},... | collective-permute-start | bytes 73736 | tf_op jit(solution)/shard_map/ppermute | solution.py:230
  4.0 0.8 %pad_maximum_fusion = bf16[32,768]{1,0:T(8,128)(2,1)S(1)} fusion(bf16[16,768]{1,0:T(8,128)(2,1)} %param.6), kind=kLoop, calls=%fused_computation | loop fusion | flops 98304 | bytes 73728 | tf_op jit(solution)/shard_map/concatenate | solution.py:232
  4.8 1.2 %collective-permute-done = bf16[16,768]{1,0:T(8,128)(2,1)S(1)} collective-permute-done((bf16[16,768]{1,0:T(8,128)(2,1)}, bf16[16,768]{1,0:T(8,128)(2,1)S(1)}, u32[]{:S(2)}, u32[]{:S(2)}) %collective-permute-start) | collective-permute-done | bytes 24608 | tf_op jit(solution)/shard_map/ppermute | solution.py:230
  6.1 0.0 copy-start
  6.1 1.2 %collective-permute-start.1 = (bf16[32,768]{1,0:T(8,128)(2,1)S(1)}, bf16[32,768]{1,0:T(8,128)(2,1)S(1)}, u32[]{:S(2)}, u32[]{:S(2)}) collective-permute-start(bf16[32,768]{1,0:T(8,128)(2,1)S(1)} %constant_dynamic-update-slice_fusion.held_ref), channel_id=1, source_target_pairs={{0,7},{1,4},{2,5},{3,6},{4,3},{5,2},{6,1},{7,0},{8,15},{9,12},{10,... | collective-permute-start | bytes 147464 | tf_op jit(solution)/shard_map/ppermute | solution.py:237
  7.3 0.5 %collective-permute-start.2 = (bf16[32,768]{1,0:T(8,128)(2,1)S(1)}, bf16[32,768]{1,0:T(8,128)(2,1)S(1)}, u32[]{:S(2)}, u32[]{:S(2)}) collective-permute-start(bf16[32,768]{1,0:T(8,128)(2,1)S(1)} %constant_dynamic-update-slice_fusion.held_ref), channel_id=1, source_target_pairs={{0,2},{1,6},{2,0},{3,4},{4,1},{5,7},{6,3},{7,5},{8,10},{9,14},{10,... | collective-permute-start | bytes 147464 | tf_op jit(solution)/shard_map/ppermute | solution.py:237
  7.8 1.2 %collective-permute-start.3 = (bf16[32,768]{1,0:T(8,128)(2,1)S(1)}, bf16[32,768]{1,0:T(8,128)(2,1)S(1)}, u32[]{:S(2)}, u32[]{:S(2)}) collective-permute-start(bf16[32,768]{1,0:T(8,128)(2,1)S(1)} %constant_dynamic-update-slice_fusion.held_ref), channel_id=1, source_target_pairs={{0,5},{1,3},{2,7},{3,1},{4,6},{5,0},{6,4},{7,2},{8,13},{9,11},{10,... | collective-permute-start | bytes 147464 | tf_op jit(solution)/shard_map/ppermute | solution.py:237
  9.0 1.4 %copy.4 = bf16[512,768]{0,1:T(8,128)(2,1)S(1)} copy(bf16[512,768]{1,0:T(8,128)(2,1)} %param.5) | data formatting | bytes 1572864 | tf_op args[0]
  10.4 0.0 copy-done
  10.4 0.3 %shard_map.37 = (s32[32,512]{1,0:T(8,128)S(1)}, f32[1,512]{1,0:T(1,128)S(1)}, f32[1,512]{1,0:T(1,128)S(1)}, f32[32,512]{1,0:T(8,128)S(1)}) custom-call(bf16[768,512]{1,0:T(8,128)(2,1)S(1)} %bitcast.3, bf16[32,768]{1,0:T(8,128)(2,1)S(1)} %constant_dynamic-update-slice_fusion.held_ref, s32[32,512]{1,0:T(8,128)S(1)} %bitcast.6), custom_call_target="tpu_custom_call" | custom-call | flops 25165824 | bytes 966656 | tf_op jit(solution)/shard_map/pallas_call | solution.py:190
  10.7 0.0 collective-permute-done.1.refs_0_
  10.7 0.3 %shard_map.38 = (f32[1,512]{1,0:T(1,128)S(1)}, f32[1,512]{1,0:T(1,128)S(1)}, f32[32,512]{1,0:T(8,128)S(1)}) custom-call(bf16[768,512]{1,0:T(8,128)(2,1)S(1)} %bitcast.4, s32[32,512]{1,0:T(8,128)S(1)} %get-tuple-element.24.local_ref, f32[1,512]{1,0:T(1,128)S(1)} %get-tuple-element.25.top_ref, f32[1,512]{1,0:T(1,128)S(1)} %get-tuple-element.26.total_ref, ...), custom_call_target="tpu_custom_call" | custom-call | flops 25165824 | bytes 966656 | tf_op jit(solution)/shard_map/pallas_call | solution.py:203
  11.1 0.5 %collective-permute-done.2.refs_0_ = bf16[32,768]{1,0:T(8,128)(2,1)S(1)} collective-permute-done((bf16[32,768]{1,0:T(8,128)(2,1)S(1)}, bf16[32,768]{1,0:T(8,128)(2,1)S(1)}, u32[]{:S(2)}, u32[]{:S(2)}) %collective-permute-start.2) | collective-permute-done | bytes 49184 | tf_op jit(solution)/shard_map/ppermute | solution.py:237
  11.5 0.0 collective-permute-done.3.refs_1_
  11.5 0.4 %shard_map.39.mine_ref = f32[40,512]{1,0:T(8,128)S(1)} custom-call(bf16[768,512]{1,0:T(8,128)(2,1)S(1)} %bitcast.5, s32[32,512]{1,0:T(8,128)S(1)} %get-tuple-element.24.local_ref, f32[1,512]{1,0:T(1,128)S(1)} %get-tuple-element.28.top_ref, f32[1,512]{1,0:T(1,128)S(1)} %get-tuple-element.29.total_ref, f32[32,512]{1,0:T(8,128)S(1)} %get-tuple-element.30.picked_ref, ...), custom_call_target="tpu_custom_call" | custom-call | flops 50331648 | bytes 1015808 | tf_op jit(solution)/shard_map/pallas_call | solution.py:203
  11.9 0.5 %collective-permute-start.4 = (f32[40,512]{1,0:T(8,128)S(1)}, f32[40,512]{1,0:T(8,128)S(1)}, u32[]{:S(2)}, u32[]{:S(2)}) collective-permute-start(f32[40,512]{1,0:T(8,128)S(1)} %shard_map.39.mine_ref), channel_id=1, source_target_pairs={{0,1},{1,0},{2,3},{3,2},{4,5},{5,4},{6,7},{7,6},{8,9},{9,8},{10,11... | collective-permute-start | bytes 245768 | tf_op jit(solution)/shard_map/ppermute | solution.py:244
  12.4 0.9 %collective-permute-done.4.other_ref = f32[40,512]{1,0:T(8,128)S(1)} collective-permute-done((f32[40,512]{1,0:T(8,128)S(1)}, f32[40,512]{1,0:T(8,128)S(1)}, u32[]{:S(2)}, u32[]{:S(2)}) %collective-permute-start.4) | collective-permute-done | bytes 81952 | tf_op jit(solution)/shard_map/ppermute | solution.py:244
  13.4 0.7 %shard_map.40 = f32[32,512]{1,0:T(8,128)} custom-call(f32[40,512]{1,0:T(8,128)S(1)} %shard_map.39.mine_ref, f32[40,512]{1,0:T(8,128)S(1)} %collective-permute-done.4.other_ref), custom_call_target="tpu_custom_call" | custom-call | tf_op jit(solution)/shard_map/pallas_call | solution.py:214
  (1 shorter events, 0.0 us)
Async XLA Ops:
  0.0 6.1 %collective-permute-start = (bf16[16,768]{1,0:T(8,128)(2,1)}, bf16[16,768]{1,0:T(8,128)(2,1)S(1)}, u32[]{:S(2)}, u32[]{:S(2)}) collective-permute-start(bf16[16,768]{1,0:T(8,128)(2,1)} %param.6), channel_id=1, source_target_pairs={{0,8},{1,9},{2,11},{3,10},{4,12},{5,13},{6,14},{7,15},{8,0},{9,1},... | collective-permute-start | bytes 73736 | tf_op jit(solution)/shard_map/ppermute | solution.py:230
  6.1 4.3 %copy-start = (s32[512,32]{0,1:T(8,128)S(1)}, s32[512,32]{0,1:T(8,128)}, u32[]{:S(2)}) copy-start(s32[512,32]{0,1:T(8,128)} %param.7) | copy-start | bytes 196612
  6.1 4.7 %collective-permute-start.1 = (bf16[32,768]{1,0:T(8,128)(2,1)S(1)}, bf16[32,768]{1,0:T(8,128)(2,1)S(1)}, u32[]{:S(2)}, u32[]{:S(2)}) collective-permute-start(bf16[32,768]{1,0:T(8,128)(2,1)S(1)} %constant_dynamic-update-slice_fusion.held_ref), channel_id=1, source_target_pairs={{0,7},{1,4},{2,5},{3,6},{4,3},{5,2},{6,1},{7,0},{8,15},{9,12},{10,... | collective-permute-start | bytes 147464 | tf_op jit(solution)/shard_map/ppermute | solution.py:237
  7.3 4.3 %collective-permute-start.2 = (bf16[32,768]{1,0:T(8,128)(2,1)S(1)}, bf16[32,768]{1,0:T(8,128)(2,1)S(1)}, u32[]{:S(2)}, u32[]{:S(2)}) collective-permute-start(bf16[32,768]{1,0:T(8,128)(2,1)S(1)} %constant_dynamic-update-slice_fusion.held_ref), channel_id=1, source_target_pairs={{0,2},{1,6},{2,0},{3,4},{4,1},{5,7},{6,3},{7,5},{8,10},{9,14},{10,... | collective-permute-start | bytes 147464 | tf_op jit(solution)/shard_map/ppermute | solution.py:237
  7.8 3.8 %collective-permute-start.3 = (bf16[32,768]{1,0:T(8,128)(2,1)S(1)}, bf16[32,768]{1,0:T(8,128)(2,1)S(1)}, u32[]{:S(2)}, u32[]{:S(2)}) collective-permute-start(bf16[32,768]{1,0:T(8,128)(2,1)S(1)} %constant_dynamic-update-slice_fusion.held_ref), channel_id=1, source_target_pairs={{0,5},{1,3},{2,7},{3,1},{4,6},{5,0},{6,4},{7,2},{8,13},{9,11},{10,... | collective-permute-start | bytes 147464 | tf_op jit(solution)/shard_map/ppermute | solution.py:237
  11.9 1.5 %collective-permute-start.4 = (f32[40,512]{1,0:T(8,128)S(1)}, f32[40,512]{1,0:T(8,128)S(1)}, u32[]{:S(2)}, u32[]{:S(2)}) collective-permute-start(f32[40,512]{1,0:T(8,128)S(1)} %shard_map.39.mine_ref), channel_id=1, source_target_pairs={{0,1},{1,0},{2,3},{3,2},{4,5},{5,4},{6,7},{7,6},{8,9},{9,8},{10,11... | collective-permute-start | bytes 245768 | tf_op jit(solution)/shard_map/ppermute | solution.py:244
